TPU v7x, 256 devices: a whole 4x4x8 slice. The times are simulated.
256 devices in a mesh: freq: 4 (over x), tile: 64 (over y, z, core).
Axes of the slice: x: 4, y: 4, z: 8, core: 2. Of those that a mesh axis runs over, the one named last changes fastest.
Arguments:
- direct_field: float32 [16, 2, 64, 16384], P('freq', None, None, 'tile'), may hold values from -6 to 6
- u_factors: bfloat16 [16, 64, 64, 2, 16, 256], P('freq', 'tile'), may hold values from -0.1875 to 0.1875
- v_factors: bfloat16 [16, 64, 64, 2, 16, 256], P('freq', None, 'tile'), may hold values from -0.25 to 0.25
- tile_ranks: int32 [16, 64, 64], P('freq', 'tile'), may hold values from 1 to 16
- onsets_source: int32 [64, 16384], P(None, 'tile'), may hold values from 32 to 223
- onsets_receiver: int32 [64, 16384], P(None, 'tile'), may hold values from 32 to 223
Outputs:
- focus_plus: float32 [16, 2, 64, 16384], P('freq', None, None, 'tile')
- focus_minus: float32 [16, 2, 64, 16384], P('freq', None, None, 'tile')
Inputs may be any that keep to these rules, and one draw needn't show every extreme that they name: Only the first tile_ranks rank rows of a tile's U and V belong to it.
All inputs are finite; a program needn't handle non-finite values.
Results may differ from a plain program's by a relative error of at most 0.0075.
Values may be sent and summed in bfloat16 or wider, within the bound.
No kernel may reach another device: no remote copies, remote signals or barrier semaphores. Data moves between devices by JAX's collectives and lax.ppermute only.
A program may use at most 128 MiB of HBM per device.

v0:
```python
import functools

import numpy as np
import jax
import jax.numpy as jnp
from jax import lax
from jax.experimental import pallas as pl
from jax.experimental.pallas import tpu as pltpu
from jax.sharding import PartitionSpec as P

TILE = 256
RMAX = 16
FOCAL = 64
SAMPLES = 256
LOWBIN = 4
ITERS = 2
TILES = 64
FREQS = 16
GROUPS = 4
OWN = FREQS // GROUPS
PW = 8
SETS = FOCAL // GROUPS // PW
VMEM_LIMIT = 48 * 1024 * 1024
BF = jnp.bfloat16
F32 = jnp.float32

FIELD = (OWN, SETS, 2 * PW, TILE)


def params():
    return pltpu.CompilerParams(vmem_limit_bytes=VMEM_LIMIT)


def dot_nt(a, b):
    return lax.dot_general(a, b, (((1,), (1,)), ((), ())), preferred_element_type=F32)


def dot_tn(a, b):
    return lax.dot_general(a, b, (((0,), (0,)), ((), ())), preferred_element_type=F32)


def focal_start(m, r, g):
    return pl.multiple_of(((m + GROUPS - r) % GROUPS * SETS + g) * PW, PW)


def project_kernel(forward, use_direct, use_field, *refs):
    refs = list(refs)
    o_ref = refs.pop()
    f_ref = refs.pop()
    if use_direct:
        m_ref, d_ref = refs[:2]
        refs = refs[2:]
    for f in range(OWN):
        plain, turned = [], []
        for r in range(GROUPS):
            for g in range(SETS):
                real = imag = None
                if use_direct:
                    at = pl.ds(focal_start(m_ref[0], r, g), PW)
                    real, imag = d_ref[f, 0, at, :], d_ref[f, 1, at, :]
                if use_field:
                    field = refs[r][f, g].astype(F32)
                    real = field[:PW] if real is None else real + field[:PW]
                    imag = field[PW:] if imag is None else imag + field[PW:]
                plain += [real, imag]
                turned += [imag, -real]
        total = None
        for part, rows in enumerate((plain, turned)):
            x = jnp.concatenate(rows, axis=0).astype(BF)
            factor = f_ref[f, :, 0, part] if forward else f_ref[f, 0, :, part]
            term = dot_nt(factor.reshape(TILES * RMAX, TILE), x)
            total = term if total is None else total + term
        o_ref[:, f] = total.astype(BF).reshape(TILES, RMAX, 2 * FOCAL)


def vmem(count=1):
    return [pl.BlockSpec(memory_space=pltpu.VMEM)] * count


def project(forward, factors, direct=None, me=None, field=None):
    ins, specs = [], []
    if direct is not None:
        ins += [me, direct]
        specs += [pl.BlockSpec(memory_space=pltpu.SMEM)] + vmem()
    if field is not None:
        ins += list(field)
        specs += vmem(GROUPS)
    return pl.pallas_call(
        functools.partial(project_kernel, forward, direct is not None, field is not None),
        in_specs=specs + vmem(),
        out_specs=vmem()[0],
        out_shape=jax.ShapeDtypeStruct((TILES, OWN, RMAX, 2 * FOCAL), BF),
        compiler_params=params(),
        cost_estimate=pl.CostEstimate(flops=600_000_000, bytes_accessed=5_000_000, transcendentals=0),
        name="project",
    )(*ins, factors)


def expand_kernel(forward, z_ref, f_ref, *outs):
    for f in range(OWN):
        z = z_ref[:, f].reshape(TILES * RMAX, 2 * FOCAL)
        straight, crossed = [
            dot_tn(z, (f_ref[f, 0, :, c] if forward else f_ref[f, :, 0, c]).reshape(TILES * RMAX, TILE))
            for c in range(2)
        ]
        for r in range(GROUPS):
            for g in range(SETS):
                at = (r * SETS + g) * 2 * PW
                real_part = straight[at : at + PW] - crossed[at + PW : at + 2 * PW]
                imag_part = straight[at + PW : at + 2 * PW] + crossed[at : at + PW]
                outs[-r % GROUPS][f, g] = jnp.concatenate([real_part, imag_part], axis=0).astype(BF)


def expand(forward, z, factors):
    return pl.pallas_call(
        functools.partial(expand_kernel, forward),
        in_specs=vmem(2),
        out_specs=vmem(GROUPS),
        out_shape=[jax.ShapeDtypeStruct(FIELD, BF)] * GROUPS,
        compiler_params=params(),
        cost_estimate=pl.CostEstimate(flops=600_000_000, bytes_accessed=5_000_000, transcendentals=0),
        name="expand",
    )(z, factors)


def window_kernel(s0, s1, s2, s3, onset_ref, t_ref, f_ref, *outs):
    rows = OWN * 2 * PW
    count = GROUPS * rows
    lane = lax.broadcasted_iota(jnp.int32, (1, count), 1) % PW
    row = lax.broadcasted_iota(jnp.int32, (count, 1), 0) % PW
    moment = lax.broadcasted_iota(jnp.int32, (SAMPLES, TILE), 0)
    fields = [
        jnp.concatenate([ref[:, g].reshape(rows, TILE) for ref in (s0, s1, s2, s3)], axis=0)
        for g in range(SETS)
    ]
    totals = [jnp.zeros((count, TILE), F32) for _ in range(SETS)]
    for p in range(PW):
        pick_lane = (lane == p).astype(F32).astype(BF)
        pick_row = (row == p).astype(F32).astype(BF)
        inverse = [t_ref[part] * pick_lane for part in range(2)]
        forward = [f_ref[part] * pick_row for part in range(2)]
        for g in range(SETS):
            trace = sum(jnp.dot(part, fields[g], preferred_element_type=F32) for part in inverse)
            limit = onset_ref[g * PW + p : g * PW + p + 1, :]
            kept = jnp.where(moment < limit, trace, 0.0).astype(BF)
            totals[g] += sum(jnp.dot(part, kept, preferred_element_type=F32) for part in forward)
    for g in range(SETS):
        result = totals[g].astype(BF)
        for r in range(GROUPS):
            outs[-r % GROUPS][:, g] = result[r * rows : (r + 1) * rows].reshape(OWN, 2 * PW, TILE)


def window(field, onset, tables):
    return pl.pallas_call(
        window_kernel,
        in_specs=vmem(GROUPS + 3),
        out_specs=vmem(GROUPS),
        out_shape=[jax.ShapeDtypeStruct(FIELD, BF)] * GROUPS,
        compiler_params=params(),
        cost_estimate=pl.CostEstimate(flops=2_200_000_000, bytes_accessed=1_000_000, transcendentals=0),
        name="window",
    )(*field, onset, *tables)


def finish_kernel(use_direct, *refs):
    refs = list(refs)
    o_ref = refs.pop()
    m_ref = refs.pop(0)
    d_ref = refs.pop(0) if use_direct else None
    for r in range(GROUPS):
        for g in range(SETS):
            at = pl.ds(focal_start(m_ref[0], r, g), PW)
            for f in range(OWN):
                field = refs[r][f, g].astype(F32)
                for c in range(2):
                    value = field[c * PW : (c + 1) * PW]
                    if use_direct:
                        value = value + d_ref[f, c, at, :]
                    o_ref[f, c, at, :] = value


def finish(me, field, direct=None):
    use_direct = direct is not None
    return pl.pallas_call(
        functools.partial(finish_kernel, use_direct),
        in_specs=[pl.BlockSpec(memory_space=pltpu.SMEM)] + vmem(use_direct + GROUPS),
        out_specs=vmem()[0],
        out_shape=jax.ShapeDtypeStruct((OWN, 2, FOCAL, TILE), F32),
        compiler_params=params(),
        cost_estimate=pl.CostEstimate(flops=1_000_000, bytes_accessed=1_000_000, transcendentals=0),
        name="finish",
    )(me, *([direct] if use_direct else []), *field)


def split_bf16(table):
    high = table.astype(jnp.bfloat16.dtype)
    return np.stack([high, (table - high.astype(np.float64)).astype(jnp.bfloat16.dtype)])


def table_constants():
    turns = (np.arange(FREQS)[:, None] + LOWBIN) * np.arange(SAMPLES)[None, :] % SAMPLES
    angles = 2.0 * np.pi / SAMPLES * turns
    paired = np.stack([np.cos(angles), -np.sin(angles)], axis=1)
    spread = np.repeat(paired.reshape(GROUPS, OWN, 2, 1, SAMPLES), PW, axis=3)
    order = [3, 2, 1, 0, 3, 2, 1]
    rows = spread[order].reshape(len(order) * OWN * 2 * PW, SAMPLES)
    return split_bf16(np.ascontiguousarray(rows.T)), split_bf16(2.0 / SAMPLES * rows)


def own_tables(me):
    inverse, forward = table_constants()
    count = FREQS * 2 * PW
    start = (GROUPS - 1 - me) * (OWN * 2 * PW)
    return (
        lax.dynamic_slice_in_dim(jnp.asarray(inverse), start, count, 2),
        lax.dynamic_slice_in_dim(jnp.asarray(forward), start, count, 1),
    )


def exchange(parts):
    steps = [
        lax.ppermute(parts[r], "freq", [(i, (i + r) % GROUPS) for i in range(GROUPS)])
        for r in range(1, GROUPS)
    ]
    return [parts[0]] + steps


def own_onsets(onsets, me):
    return lax.dynamic_slice_in_dim(onsets, me * (SETS * PW), SETS * PW, 0)


def route(z):
    return lax.all_to_all(
        z.reshape(TILES, OWN * RMAX, 2 * FOCAL), "tile", 0, 0, tiled=True
    ).reshape(z.shape)


def per_device(direct_field, u_factors, v_factors, tile_ranks, onsets_source, onsets_receiver):
    me = lax.axis_index("freq")
    index = me.reshape(1).astype(jnp.int32)
    tables = own_tables(me)
    sources, receivers = own_onsets(onsets_source, me), own_onsets(onsets_receiver, me)
    inside = lax.broadcasted_iota(jnp.int32, (1, 1, 1, 1, RMAX, 1), 4)
    u_own = u_factors * (inside < tile_ranks[:, :, :, None, None, None]).astype(BF)

    plus = None
    for _ in range(ITERS):
        z = project(True, v_factors, direct_field, index, plus)
        image = exchange(expand(True, route(z), u_own))
        minus = exchange(window(image, sources, tables))
        w = project(False, u_own, field=minus)
        image = exchange(expand(False, route(w), v_factors))
        plus = exchange(window(image, receivers, tables))
    return (finish(index, plus, direct_field), finish(index, minus))


def solution(mesh):
    return jax.shard_map(
        per_device,
        mesh=mesh,
        in_specs=(
            P("freq", None, None, "tile"),
            P("freq", "tile", None, None, None, None),
            P("freq", None, "tile", None, None, None),
            P("freq", "tile", None),
            P(None, "tile"),
            P(None, "tile"),
        ),
        out_specs=(P("freq", None, None, "tile"), P("freq", None, None, "tile")),
        check_vma=False,
    )
```

profile of v0, /device:TPU:8, one launch (start us, length us, event | category | flops | bytes accessed | tf_op | source)
XLA Modules:
  0.0 246.6 jit_solution(8843670265866461936)
XLA Ops:
  0.7 2.2 copy-done.3
  2.9 1.0 copy-done.7
  3.9 2.3 project.4
  6.2 12.1 %all-to-all-start = ((bf16[64,64,128]{2,1,0:T(8,128)(2,1)}), bf16[64,64,128]{2,1,0:T(8,128)(2,1)S(1)}, u32[]{:S(2)}, u32[]{:S(2)}) async-start(bf16[64,64,128]{2,1,0:T(8,128)(2,1)} %bitcast.1), calls=%async_computation | async-start | bytes 2097152 | tf_op jit(solution)/shard_map/all_to_all | solution.py:233
  18.6 3.9 %broadcast_multiply_fusion.f_ref.refs_4_ = bf16[4,1,64,2,16,256]{5,4,3,2,1,0:T(8,128)(2,1)} fusion(bf16[4,1,64,2,16,256]{5,4,3,2,1,0:T(8,128)(2,1)} %param.9, bf16[4,64,16]{2,1,0:T(8,128)(2,1)S(1)} %fusion), kind=kLoop, calls=%fused_computation | loop fusion | flops 2097152 | bytes 8396800 | tf_op jit(solution)/shard_map/mul | solution.py:244
  22.5 22.9 %all-to-all-done = bf16[64,64,128]{2,1,0:T(8,128)(2,1)S(1)} async-done(((bf16[64,64,128]{2,1,0:T(8,128)(2,1)}), bf16[64,64,128]{2,1,0:T(8,128)(2,1)S(1)}, u32[]{:S(2)}, u32[]{:S(2)}) %all-to-all-start) | async-done | bytes 1048608 | tf_op jit(solution)/shard_map/all_to_all | solution.py:233
  45.4 2.2 copy-done.1
  48.4 1.6 collective-permute-start
  49.9 2.7 %collective-permute-start.1 = (bf16[4,2,16,256]{3,2,1,0:T(8,128)(2,1)S(1)}, bf16[4,2,16,256]{3,2,1,0:T(8,128)(2,1)S(1)}, u32[]{:S(2)}, u32[]{:S(2)}) collective-permute-start(bf16[4,2,16,256]{3,2,1,0:T(8,128)(2,1)S(1)} %get-tuple-element.36), channel_id=1, source_target_pairs={{0,128},{64,192},{128,0},{192,64},{1,129},{65,193},{129,1},{193,65... | collective-permute-start | bytes 196616 | tf_op jit(solution)/shard_map/ppermute | solution.py:222
  52.7 1.4 collective-permute-start.2
  54.3 2.4 collective-permute-done.1.s2
  57.5 2.6 %window.4 = (bf16[4,2,16,256]{3,2,1,0:T(8,128)(2,1)S(1)}, bf16[4,2,16,256]{3,2,1,0:T(8,128)(2,1)S(1)}, bf16[4,2,16,256]{3,2,1,0:T(8,128)(2,1)S(1)}, bf16[4,2,16,256]{3,2,1,0:T(8,128)(2,1)S(1)}) custom-call(bf16[4,2,16,256]{3,2,1,0:T(8,128)(2,1)S(1)} %get-tuple-element.34.s0, bf16[4,2,16,256]{3,2,1,0:T(8,128)(2,1)S(1)} %collective-permute-done.s1, ...), custom_call_target="tpu_custom_call" | custom-call | flops 2200000000 | bytes 1000000 | tf_op jit(solution)/shard_map/window/pallas_call | solution.py:154
  60.1 1.4 collective-permute-start.3
  61.5 2.8 %collective-permute-start.4 = (bf16[4,2,16,256]{3,2,1,0:T(8,128)(2,1)S(1)}, bf16[4,2,16,256]{3,2,1,0:T(8,128)(2,1)S(1)}, u32[]{:S(2)}, u32[]{:S(2)}) collective-permute-start(bf16[4,2,16,256]{3,2,1,0:T(8,128)(2,1)S(1)} %get-tuple-element.40), channel_id=1, source_target_pairs={{0,128},{64,192},{128,0},{192,64},{1,129},{65,193},{129,1},{193,65... | collective-permute-start | bytes 196616 | tf_op jit(solution)/shard_map/ppermute | solution.py:222
  66.1 1.6 collective-permute-done.4.refs_2_
  68.6 1.2 project.5
  69.8 34.2 %all_to_all.20 = bf16[64,64,128]{2,1,0:T(8,128)(2,1)S(1)} all-to-all(bf16[64,64,128]{2,1,0:T(8,128)(2,1)S(1)} %bitcast.14), channel_id=1, replica_groups=mesh['freq'=4,'tile'=64] {'tile'}, dimensions={0} | all-to-all | bytes 2097152 | tf_op jit(solution)/shard_map/all_to_all | solution.py:233
  104.9 2.9 %collective-permute-start.7 = (bf16[4,2,16,256]{3,2,1,0:T(8,128)(2,1)S(1)}, bf16[4,2,16,256]{3,2,1,0:T(8,128)(2,1)S(1)}, u32[]{:S(2)}, u32[]{:S(2)}) collective-permute-start(bf16[4,2,16,256]{3,2,1,0:T(8,128)(2,1)S(1)} %get-tuple-element.44), channel_id=1, source_target_pairs={{0,128},{64,192},{128,0},{192,64},{1,129},{65,193},{129,1},{193,65... | collective-permute-start | bytes 196616 | tf_op jit(solution)/shard_map/ppermute | solution.py:222
  107.8 1.2 collective-permute-start.8
  109.7 1.3 collective-permute-done.6.s1
  111.9 1.3 collective-permute-done.8.s3
  113.1 2.6 %window.5 = (bf16[4,2,16,256]{3,2,1,0:T(8,128)(2,1)S(1)}, bf16[4,2,16,256]{3,2,1,0:T(8,128)(2,1)S(1)}, bf16[4,2,16,256]{3,2,1,0:T(8,128)(2,1)S(1)}, bf16[4,2,16,256]{3,2,1,0:T(8,128)(2,1)S(1)}) custom-call(bf16[4,2,16,256]{3,2,1,0:T(8,128)(2,1)S(1)} %get-tuple-element.42.s0, bf16[4,2,16,256]{3,2,1,0:T(8,128)(2,1)S(1)} %collective-permute-done.6.s1, ...), custom_call_target="tpu_custom_call" | custom-call | flops 2200000000 | bytes 1000000 | tf_op jit(solution)/shard_map/window/pallas_call | solution.py:154
  115.8 1.2 collective-permute-start.9
  116.9 3.2 %collective-permute-start.10 = (bf16[4,2,16,256]{3,2,1,0:T(8,128)(2,1)S(1)}, bf16[4,2,16,256]{3,2,1,0:T(8,128)(2,1)S(1)}, u32[]{:S(2)}, u32[]{:S(2)}) collective-permute-start(bf16[4,2,16,256]{3,2,1,0:T(8,128)(2,1)S(1)} %get-tuple-element.48), channel_id=1, source_target_pairs={{0,128},{64,192},{128,0},{192,64},{1,129},{65,193},{129,1},{193,65... | collective-permute-start | bytes 196616 | tf_op jit(solution)/shard_map/ppermute | solution.py:222
  120.1 1.2 collective-permute-done.9.refs_3_
  121.3 2.3 collective-permute-done.10.refs_4_
  124.4 2.2 copy-done.5
  126.6 1.3 project.6
  127.9 33.3 %all_to_all.21 = bf16[64,64,128]{2,1,0:T(8,128)(2,1)S(1)} all-to-all(bf16[64,64,128]{2,1,0:T(8,128)(2,1)S(1)} %bitcast.15), channel_id=1, replica_groups=mesh['freq'=4,'tile'=64] {'tile'}, dimensions={0} | all-to-all | bytes 2097152 | tf_op jit(solution)/shard_map/all_to_all | solution.py:233
  162.0 2.9 %collective-permute-start.13 = (bf16[4,2,16,256]{3,2,1,0:T(8,128)(2,1)S(1)}, bf16[4,2,16,256]{3,2,1,0:T(8,128)(2,1)S(1)}, u32[]{:S(2)}, u32[]{:S(2)}) collective-permute-start(bf16[4,2,16,256]{3,2,1,0:T(8,128)(2,1)S(1)} %get-tuple-element.52), channel_id=1, source_target_pairs={{0,128},{64,192},{128,0},{192,64},{1,129},{65,193},{129,1},{193,65... | collective-permute-start | bytes 196616 | tf_op jit(solution)/shard_map/ppermute | solution.py:222
  164.8 10.7 %collective-permute-start.14 = (bf16[4,2,16,256]{3,2,1,0:T(8,128)(2,1)S(1)}, bf16[4,2,16,256]{3,2,1,0:T(8,128)(2,1)S(1)}, u32[]{:S(2)}, u32[]{:S(2)}) collective-permute-start(bf16[4,2,16,256]{3,2,1,0:T(8,128)(2,1)S(1)} %get-tuple-element.53), channel_id=1, source_target_pairs={{0,192},{64,0},{128,64},{192,128},{1,193},{65,1},{129,65},{193,129... | collective-permute-start | bytes 196616 | tf_op jit(solution)/shard_map/ppermute | solution.py:222
  175.5 3.6 %collective-permute-done.14.s3 = bf16[4,2,16,256]{3,2,1,0:T(8,128)(2,1)S(1)} collective-permute-done((bf16[4,2,16,256]{3,2,1,0:T(8,128)(2,1)S(1)}, bf16[4,2,16,256]{3,2,1,0:T(8,128)(2,1)S(1)}, u32[]{:S(2)}, u32[]{:S(2)}) %collective-permute-start.14) | collective-permute-done | bytes 65568 | tf_op jit(solution)/shard_map/ppermute | solution.py:222
  179.1 2.6 %window.6 = (bf16[4,2,16,256]{3,2,1,0:T(8,128)(2,1)S(1)}, bf16[4,2,16,256]{3,2,1,0:T(8,128)(2,1)S(1)}, bf16[4,2,16,256]{3,2,1,0:T(8,128)(2,1)S(1)}, bf16[4,2,16,256]{3,2,1,0:T(8,128)(2,1)S(1)}) custom-call(bf16[4,2,16,256]{3,2,1,0:T(8,128)(2,1)S(1)} %get-tuple-element.50.s0, bf16[4,2,16,256]{3,2,1,0:T(8,128)(2,1)S(1)} %collective-permute-done.12.s1, ...), custom_call_target="tpu_custom_call" | custom-call | flops 2200000000 | bytes 1000000 | tf_op jit(solution)/shard_map/window/pallas_call | solution.py:154
  181.7 1.3 collective-permute-start.15
  183.0 2.7 %collective-permute-start.16 = (bf16[4,2,16,256]{3,2,1,0:T(8,128)(2,1)S(1)}, bf16[4,2,16,256]{3,2,1,0:T(8,128)(2,1)S(1)}, u32[]{:S(2)}, u32[]{:S(2)}) collective-permute-start(bf16[4,2,16,256]{3,2,1,0:T(8,128)(2,1)S(1)} %get-tuple-element.56), channel_id=1, source_target_pairs={{0,128},{64,192},{128,0},{192,64},{1,129},{65,193},{129,1},{193,65... | collective-permute-start | bytes 196616 | tf_op jit(solution)/shard_map/ppermute | solution.py:222
  185.8 2.0 collective-permute-done.15.refs_1_.refs_2_
  187.8 1.3 collective-permute-done.16.refs_2_.refs_3_
  190.0 1.2 project.7
  191.3 34.0 %all_to_all.22 = bf16[64,64,128]{2,1,0:T(8,128)(2,1)S(1)} all-to-all(bf16[64,64,128]{2,1,0:T(8,128)(2,1)S(1)} %bitcast.16), channel_id=1, replica_groups=mesh['freq'=4,'tile'=64] {'tile'}, dimensions={0} | all-to-all | bytes 2097152 | tf_op jit(solution)/shard_map/all_to_all | solution.py:233
  226.2 2.8 %collective-permute-start.19 = (bf16[4,2,16,256]{3,2,1,0:T(8,128)(2,1)S(1)}, bf16[4,2,16,256]{3,2,1,0:T(8,128)(2,1)S(1)}, u32[]{:S(2)}, u32[]{:S(2)}) collective-permute-start(bf16[4,2,16,256]{3,2,1,0:T(8,128)(2,1)S(1)} %get-tuple-element.60), channel_id=1, source_target_pairs={{0,128},{64,192},{128,0},{192,64},{1,129},{65,193},{129,1},{193,65... | collective-permute-start | bytes 196616 | tf_op jit(solution)/shard_map/ppermute | solution.py:222
  229.0 1.2 collective-permute-start.20
  230.2 1.9 collective-permute-done.18.s1
  232.1 1.0 collective-permute-done.19.s2
  233.1 1.2 collective-permute-done.20.s3
  234.3 2.6 %window.7 = (bf16[4,2,16,256]{3,2,1,0:T(8,128)(2,1)S(1)}, bf16[4,2,16,256]{3,2,1,0:T(8,128)(2,1)S(1)}, bf16[4,2,16,256]{3,2,1,0:T(8,128)(2,1)S(1)}, bf16[4,2,16,256]{3,2,1,0:T(8,128)(2,1)S(1)}) custom-call(bf16[4,2,16,256]{3,2,1,0:T(8,128)(2,1)S(1)} %get-tuple-element.58.s0, bf16[4,2,16,256]{3,2,1,0:T(8,128)(2,1)S(1)} %collective-permute-done.18.s1, ...), custom_call_target="tpu_custom_call" | custom-call | flops 2200000000 | bytes 1000000 | tf_op jit(solution)/shard_map/window/pallas_call | solution.py:154
  236.9 1.1 collective-permute-start.21
  238.1 3.2 %collective-permute-start.22 = (bf16[4,2,16,256]{3,2,1,0:T(8,128)(2,1)S(1)}, bf16[4,2,16,256]{3,2,1,0:T(8,128)(2,1)S(1)}, u32[]{:S(2)}, u32[]{:S(2)}) collective-permute-start(bf16[4,2,16,256]{3,2,1,0:T(8,128)(2,1)S(1)} %get-tuple-element.64), channel_id=1, source_target_pairs={{0,128},{64,192},{128,0},{192,64},{1,129},{65,193},{129,1},{193,65... | collective-permute-start | bytes 196616 | tf_op jit(solution)/shard_map/ppermute | solution.py:222
  242.5 2.3 collective-permute-done.22.refs_4_
  (48 shorter events, 13.4 us)
Async XLA Ops:
  0.6 53.5 %copy-start = (s32[64,256]{1,0:T(8,128)S(1)}, s32[64,256]{1,0:T(8,128)}, u32[]{:S(2)}) copy-start(s32[64,256]{1,0:T(8,128)} %param.12) | copy-start | bytes 196612
  0.6 2.2 copy-start.3
  2.9 1.0 copy-start.7
  3.9 14.4 %copy-start.9 = (bf16[2,448,256]{2,1,0:T(8,128)(2,1)S(1)}, bf16[2,448,256]{2,1,0:T(8,128)(2,1)}, u32[]{:S(2)}) copy-start(bf16[2,448,256]{2,1,0:T(8,128)(2,1)} %constant.21.clone) | copy-start | bytes 1376260
  3.9 14.4 %copy-start.10 = (bf16[2,256,448]{2,1,0:T(8,128)(2,1)S(1)}, bf16[2,256,448]{2,1,0:T(8,128)(2,1)}, u32[]{:S(2)}) copy-start(bf16[2,256,448]{2,1,0:T(8,128)(2,1)} %constant.20.clone) | copy-start | bytes 1376260
  3.9 14.6 %copy-start.11 = (s32[4,1,64]{2,1,0:T(1,128)S(1)}, s32[4,1,64]{2,1,0:T(1,128)}, u32[]{:S(2)}) copy-start(s32[4,1,64]{2,1,0:T(1,128)} %param.11) | copy-start | bytes 3076
  6.2 39.2 %all-to-all-start = ((bf16[64,64,128]{2,1,0:T(8,128)(2,1)}), bf16[64,64,128]{2,1,0:T(8,128)(2,1)S(1)}, u32[]{:S(2)}, u32[]{:S(2)}) async-start(bf16[64,64,128]{2,1,0:T(8,128)(2,1)} %bitcast.1), calls=%async_computation | async-start | bytes 2097152 | tf_op jit(solution)/shard_map/all_to_all | solution.py:233
  45.4 2.2 copy-start.1
  48.4 20.2 %copy-start.2 = (bf16[4,1,64,2,16,256]{5,4,3,2,1,0:T(8,128)(2,1)S(1)}, bf16[4,1,64,2,16,256]{5,4,3,2,1,0:T(8,128)(2,1)}, u32[]{:S(2)}) copy-start(bf16[4,1,64,2,16,256]{5,4,3,2,1,0:T(8,128)(2,1)} %broadcast_multiply_fusion.f_ref.refs_4_) | copy-start | bytes 12582916
  48.4 5.9 %collective-permute-start = (bf16[4,2,16,256]{3,2,1,0:T(8,128)(2,1)S(1)}, bf16[4,2,16,256]{3,2,1,0:T(8,128)(2,1)S(1)}, u32[]{:S(2)}, u32[]{:S(2)}) collective-permute-start(bf16[4,2,16,256]{3,2,1,0:T(8,128)(2,1)S(1)} %get-tuple-element.35), channel_id=1, source_target_pairs={{0,64},{64,128},{128,192},{192,0},{1,65},{65,129},{129,193},{193,1... | collective-permute-start | bytes 196616 | tf_op jit(solution)/shard_map/ppermute | solution.py:222
  49.9 6.7 %collective-permute-start.1 = (bf16[4,2,16,256]{3,2,1,0:T(8,128)(2,1)S(1)}, bf16[4,2,16,256]{3,2,1,0:T(8,128)(2,1)S(1)}, u32[]{:S(2)}, u32[]{:S(2)}) collective-permute-start(bf16[4,2,16,256]{3,2,1,0:T(8,128)(2,1)S(1)} %get-tuple-element.36), channel_id=1, source_target_pairs={{0,128},{64,192},{128,0},{192,64},{1,129},{65,193},{129,1},{193,65... | collective-permute-start | bytes 196616 | tf_op jit(solution)/shard_map/ppermute | solution.py:222
  52.7 4.8 %collective-permute-start.2 = (bf16[4,2,16,256]{3,2,1,0:T(8,128)(2,1)S(1)}, bf16[4,2,16,256]{3,2,1,0:T(8,128)(2,1)S(1)}, u32[]{:S(2)}, u32[]{:S(2)}) collective-permute-start(bf16[4,2,16,256]{3,2,1,0:T(8,128)(2,1)S(1)} %get-tuple-element.37), channel_id=1, source_target_pairs={{0,192},{64,0},{128,64},{192,128},{1,193},{65,1},{129,65},{193,129... | collective-permute-start | bytes 196616 | tf_op jit(solution)/shard_map/ppermute | solution.py:222
  60.1 43.9 %copy-start.4 = (bf16[4,64,1,2,16,256]{5,4,3,2,1,0:T(8,128)(2,1)S(1)}, bf16[4,64,1,2,16,256]{5,4,3,2,1,0:T(8,128)(2,1)}, u32[]{:S(2)}) copy-start(bf16[4,64,1,2,16,256]{5,4,3,2,1,0:T(8,128)(2,1)} %f_ref.3) | copy-start | bytes 12582916
  60.1 5.9 %collective-permute-start.3 = (bf16[4,2,16,256]{3,2,1,0:T(8,128)(2,1)S(1)}, bf16[4,2,16,256]{3,2,1,0:T(8,128)(2,1)S(1)}, u32[]{:S(2)}, u32[]{:S(2)}) collective-permute-start(bf16[4,2,16,256]{3,2,1,0:T(8,128)(2,1)S(1)} %get-tuple-element.39), channel_id=1, source_target_pairs={{0,64},{64,128},{128,192},{192,0},{1,65},{65,129},{129,193},{193,1... | collective-permute-start | bytes 196616 | tf_op jit(solution)/shard_map/ppermute | solution.py:222
  61.5 6.2 %collective-permute-start.4 = (bf16[4,2,16,256]{3,2,1,0:T(8,128)(2,1)S(1)}, bf16[4,2,16,256]{3,2,1,0:T(8,128)(2,1)S(1)}, u32[]{:S(2)}, u32[]{:S(2)}) collective-permute-start(bf16[4,2,16,256]{3,2,1,0:T(8,128)(2,1)S(1)} %get-tuple-element.40), channel_id=1, source_target_pairs={{0,128},{64,192},{128,0},{192,64},{1,129},{65,193},{129,1},{193,65... | collective-permute-start | bytes 196616 | tf_op jit(solution)/shard_map/ppermute | solution.py:222
  64.3 4.3 %collective-permute-start.5 = (bf16[4,2,16,256]{3,2,1,0:T(8,128)(2,1)S(1)}, bf16[4,2,16,256]{3,2,1,0:T(8,128)(2,1)S(1)}, u32[]{:S(2)}, u32[]{:S(2)}) collective-permute-start(bf16[4,2,16,256]{3,2,1,0:T(8,128)(2,1)S(1)} %get-tuple-element.41), channel_id=1, source_target_pairs={{0,192},{64,0},{128,64},{192,128},{1,193},{65,1},{129,65},{193,129... | collective-permute-start | bytes 196616 | tf_op jit(solution)/shard_map/ppermute | solution.py:222
  104.8 19.6 %copy-start.8 = (f32[4,2,64,256]{3,2,1,0:T(8,128)S(1)}, f32[4,2,64,256]{3,2,1,0:T(8,128)}, u32[]{:S(2)}) copy-start(f32[4,2,64,256]{3,2,1,0:T(8,128)} %refs_1_.5) | copy-start | bytes 1572868
  104.8 6.2 %collective-permute-start.6 = (bf16[4,2,16,256]{3,2,1,0:T(8,128)(2,1)S(1)}, bf16[4,2,16,256]{3,2,1,0:T(8,128)(2,1)S(1)}, u32[]{:S(2)}, u32[]{:S(2)}) collective-permute-start(bf16[4,2,16,256]{3,2,1,0:T(8,128)(2,1)S(1)} %get-tuple-element.43), channel_id=1, source_target_pairs={{0,64},{64,128},{128,192},{192,0},{1,65},{65,129},{129,193},{193,1... | collective-permute-start | bytes 196616 | tf_op jit(solution)/shard_map/ppermute | solution.py:222
  104.9 7.0 %collective-permute-start.7 = (bf16[4,2,16,256]{3,2,1,0:T(8,128)(2,1)S(1)}, bf16[4,2,16,256]{3,2,1,0:T(8,128)(2,1)S(1)}, u32[]{:S(2)}, u32[]{:S(2)}) collective-permute-start(bf16[4,2,16,256]{3,2,1,0:T(8,128)(2,1)S(1)} %get-tuple-element.44), channel_id=1, source_target_pairs={{0,128},{64,192},{128,0},{192,64},{1,129},{65,193},{129,1},{193,65... | collective-permute-start | bytes 196616 | tf_op jit(solution)/shard_map/ppermute | solution.py:222
  107.8 5.4 %collective-permute-start.8 = (bf16[4,2,16,256]{3,2,1,0:T(8,128)(2,1)S(1)}, bf16[4,2,16,256]{3,2,1,0:T(8,128)(2,1)S(1)}, u32[]{:S(2)}, u32[]{:S(2)}) collective-permute-start(bf16[4,2,16,256]{3,2,1,0:T(8,128)(2,1)S(1)} %get-tuple-element.45), channel_id=1, source_target_pairs={{0,192},{64,0},{128,64},{192,128},{1,193},{65,1},{129,65},{193,129... | collective-permute-start | bytes 196616 | tf_op jit(solution)/shard_map/ppermute | solution.py:222
  115.8 5.6 %collective-permute-start.9 = (bf16[4,2,16,256]{3,2,1,0:T(8,128)(2,1)S(1)}, bf16[4,2,16,256]{3,2,1,0:T(8,128)(2,1)S(1)}, u32[]{:S(2)}, u32[]{:S(2)}) collective-permute-start(bf16[4,2,16,256]{3,2,1,0:T(8,128)(2,1)S(1)} %get-tuple-element.47), channel_id=1, source_target_pairs={{0,64},{64,128},{128,192},{192,0},{1,65},{65,129},{129,193},{193,1... | collective-permute-start | bytes 196616 | tf_op jit(solution)/shard_map/ppermute | solution.py:222
  116.9 6.7 %collective-permute-start.10 = (bf16[4,2,16,256]{3,2,1,0:T(8,128)(2,1)S(1)}, bf16[4,2,16,256]{3,2,1,0:T(8,128)(2,1)S(1)}, u32[]{:S(2)}, u32[]{:S(2)}) collective-permute-start(bf16[4,2,16,256]{3,2,1,0:T(8,128)(2,1)S(1)} %get-tuple-element.48), channel_id=1, source_target_pairs={{0,128},{64,192},{128,0},{192,64},{1,129},{65,193},{129,1},{193,65... | collective-permute-start | bytes 196616 | tf_op jit(solution)/shard_map/ppermute | solution.py:222
  120.1 4.3 %collective-permute-start.11 = (bf16[4,2,16,256]{3,2,1,0:T(8,128)(2,1)S(1)}, bf16[4,2,16,256]{3,2,1,0:T(8,128)(2,1)S(1)}, u32[]{:S(2)}, u32[]{:S(2)}) collective-permute-start(bf16[4,2,16,256]{3,2,1,0:T(8,128)(2,1)S(1)} %get-tuple-element.49), channel_id=1, source_target_pairs={{0,192},{64,0},{128,64},{192,128},{1,193},{65,1},{129,65},{193,129... | collective-permute-start | bytes 196616 | tf_op jit(solution)/shard_map/ppermute | solution.py:222
  124.4 2.2 copy-start.5
  161.9 13.7 %collective-permute-start.12 = (bf16[4,2,16,256]{3,2,1,0:T(8,128)(2,1)S(1)}, bf16[4,2,16,256]{3,2,1,0:T(8,128)(2,1)S(1)}, u32[]{:S(2)}, u32[]{:S(2)}) collective-permute-start(bf16[4,2,16,256]{3,2,1,0:T(8,128)(2,1)S(1)} %get-tuple-element.51), channel_id=1, source_target_pairs={{0,64},{64,128},{128,192},{192,0},{1,65},{65,129},{129,193},{193,1... | collective-permute-start | bytes 196616 | tf_op jit(solution)/shard_map/ppermute | solution.py:222
  162.0 13.6 %collective-permute-start.13 = (bf16[4,2,16,256]{3,2,1,0:T(8,128)(2,1)S(1)}, bf16[4,2,16,256]{3,2,1,0:T(8,128)(2,1)S(1)}, u32[]{:S(2)}, u32[]{:S(2)}) collective-permute-start(bf16[4,2,16,256]{3,2,1,0:T(8,128)(2,1)S(1)} %get-tuple-element.52), channel_id=1, source_target_pairs={{0,128},{64,192},{128,0},{192,64},{1,129},{65,193},{129,1},{193,65... | collective-permute-start | bytes 196616 | tf_op jit(solution)/shard_map/ppermute | solution.py:222
  164.8 14.3 %collective-permute-start.14 = (bf16[4,2,16,256]{3,2,1,0:T(8,128)(2,1)S(1)}, bf16[4,2,16,256]{3,2,1,0:T(8,128)(2,1)S(1)}, u32[]{:S(2)}, u32[]{:S(2)}) collective-permute-start(bf16[4,2,16,256]{3,2,1,0:T(8,128)(2,1)S(1)} %get-tuple-element.53), channel_id=1, source_target_pairs={{0,192},{64,0},{128,64},{192,128},{1,193},{65,1},{129,65},{193,129... | collective-permute-start | bytes 196616 | tf_op jit(solution)/shard_map/ppermute | solution.py:222
  181.7 43.5 %copy-start.6 = (bf16[4,64,1,2,16,256]{5,4,3,2,1,0:T(8,128)(2,1)S(1)}, bf16[4,64,1,2,16,256]{5,4,3,2,1,0:T(8,128)(2,1)}, u32[]{:S(2)}) copy-start(bf16[4,64,1,2,16,256]{5,4,3,2,1,0:T(8,128)(2,1)} %f_ref.3) | copy-start | bytes 12582916
  181.7 6.1 %collective-permute-start.15 = (bf16[4,2,16,256]{3,2,1,0:T(8,128)(2,1)S(1)}, bf16[4,2,16,256]{3,2,1,0:T(8,128)(2,1)S(1)}, u32[]{:S(2)}, u32[]{:S(2)}) collective-permute-start(bf16[4,2,16,256]{3,2,1,0:T(8,128)(2,1)S(1)} %get-tuple-element.55), channel_id=1, source_target_pairs={{0,64},{64,128},{128,192},{192,0},{1,65},{65,129},{129,193},{193,1... | collective-permute-start | bytes 196616 | tf_op jit(solution)/shard_map/ppermute | solution.py:222
  183.0 6.1 %collective-permute-start.16 = (bf16[4,2,16,256]{3,2,1,0:T(8,128)(2,1)S(1)}, bf16[4,2,16,256]{3,2,1,0:T(8,128)(2,1)S(1)}, u32[]{:S(2)}, u32[]{:S(2)}) collective-permute-start(bf16[4,2,16,256]{3,2,1,0:T(8,128)(2,1)S(1)} %get-tuple-element.56), channel_id=1, source_target_pairs={{0,128},{64,192},{128,0},{192,64},{1,129},{65,193},{129,1},{193,65... | collective-permute-start | bytes 196616 | tf_op jit(solution)/shard_map/ppermute | solution.py:222
  185.8 4.3 %collective-permute-start.17 = (bf16[4,2,16,256]{3,2,1,0:T(8,128)(2,1)S(1)}, bf16[4,2,16,256]{3,2,1,0:T(8,128)(2,1)S(1)}, u32[]{:S(2)}, u32[]{:S(2)}) collective-permute-start(bf16[4,2,16,256]{3,2,1,0:T(8,128)(2,1)S(1)} %get-tuple-element.57), channel_id=1, source_target_pairs={{0,192},{64,0},{128,64},{192,128},{1,193},{65,1},{129,65},{193,129... | collective-permute-start | bytes 196616 | tf_op jit(solution)/shard_map/ppermute | solution.py:222
  226.0 6.2 %collective-permute-start.18 = (bf16[4,2,16,256]{3,2,1,0:T(8,128)(2,1)S(1)}, bf16[4,2,16,256]{3,2,1,0:T(8,128)(2,1)S(1)}, u32[]{:S(2)}, u32[]{:S(2)}) collective-permute-start(bf16[4,2,16,256]{3,2,1,0:T(8,128)(2,1)S(1)} %get-tuple-element.59), channel_id=1, source_target_pairs={{0,64},{64,128},{128,192},{192,0},{1,65},{65,129},{129,193},{193,1... | collective-permute-start | bytes 196616 | tf_op jit(solution)/shard_map/ppermute | solution.py:222
  226.2 6.9 %collective-permute-start.19 = (bf16[4,2,16,256]{3,2,1,0:T(8,128)(2,1)S(1)}, bf16[4,2,16,256]{3,2,1,0:T(8,128)(2,1)S(1)}, u32[]{:S(2)}, u32[]{:S(2)}) collective-permute-start(bf16[4,2,16,256]{3,2,1,0:T(8,128)(2,1)S(1)} %get-tuple-element.60), channel_id=1, source_target_pairs={{0,128},{64,192},{128,0},{192,64},{1,129},{65,193},{129,1},{193,65... | collective-permute-start | bytes 196616 | tf_op jit(solution)/shard_map/ppermute | solution.py:222
  229.0 5.3 %collective-permute-start.20 = (bf16[4,2,16,256]{3,2,1,0:T(8,128)(2,1)S(1)}, bf16[4,2,16,256]{3,2,1,0:T(8,128)(2,1)S(1)}, u32[]{:S(2)}, u32[]{:S(2)}) collective-permute-start(bf16[4,2,16,256]{3,2,1,0:T(8,128)(2,1)S(1)} %get-tuple-element.61), channel_id=1, source_target_pairs={{0,192},{64,0},{128,64},{192,128},{1,193},{65,1},{129,65},{193,129... | collective-permute-start | bytes 196616 | tf_op jit(solution)/shard_map/ppermute | solution.py:222
  236.9 5.6 %collective-permute-start.21 = (bf16[4,2,16,256]{3,2,1,0:T(8,128)(2,1)S(1)}, bf16[4,2,16,256]{3,2,1,0:T(8,128)(2,1)S(1)}, u32[]{:S(2)}, u32[]{:S(2)}) collective-permute-start(bf16[4,2,16,256]{3,2,1,0:T(8,128)(2,1)S(1)} %get-tuple-element.63), channel_id=1, source_target_pairs={{0,64},{64,128},{128,192},{192,0},{1,65},{65,129},{129,193},{193,1... | collective-permute-start | bytes 196616 | tf_op jit(solution)/shard_map/ppermute | solution.py:222
  238.1 6.7 %collective-permute-start.22 = (bf16[4,2,16,256]{3,2,1,0:T(8,128)(2,1)S(1)}, bf16[4,2,16,256]{3,2,1,0:T(8,128)(2,1)S(1)}, u32[]{:S(2)}, u32[]{:S(2)}) collective-permute-start(bf16[4,2,16,256]{3,2,1,0:T(8,128)(2,1)S(1)} %get-tuple-element.64), channel_id=1, source_target_pairs={{0,128},{64,192},{128,0},{192,64},{1,129},{65,193},{129,1},{193,65... | collective-permute-start | bytes 196616 | tf_op jit(solution)/shard_map/ppermute | solution.py:222
  241.3 4.3 %collective-permute-start.23 = (bf16[4,2,16,256]{3,2,1,0:T(8,128)(2,1)S(1)}, bf16[4,2,16,256]{3,2,1,0:T(8,128)(2,1)S(1)}, u32[]{:S(2)}, u32[]{:S(2)}) collective-permute-start(bf16[4,2,16,256]{3,2,1,0:T(8,128)(2,1)S(1)} %get-tuple-element.65), channel_id=1, source_target_pairs={{0,192},{64,0},{128,64},{192,128},{1,193},{65,1},{129,65},{193,129... | collective-permute-start | bytes 196616 | tf_op jit(solution)/shard_map/ppermute | solution.py:222
where the time goes:
time: 251 us; the launch traced here: 247 us
  blocking collectives  101 us (40%)
  starting transfers between devices  57.7 us (23%)
  waiting for transfers between devices  52.8 us (21%)
  Pallas kernels  21 us (8%)
  local copies, waits for them, and re-layouts  8.54 us (3%)
  other arithmetic  4.01 us (2%)
    all_to_all x3, blocking collectives, route(): lax.all_to_all(z.reshape(TILES, OWN * RMAX, 2 * FOCAL), 'tile', 0, 0, til...  101 us
    ppermute x24, starting transfers between devices, exchange(): lax.ppermute(parts[r], 'freq', [(i, (i + r) % GROUPS) for i in range(GROU...  45.6 us
    ppermute x24, waiting for transfers between devices, exchange(): lax.ppermute(parts[r], 'freq', [(i, (i + r) % GROUPS) for i in range(GROU...  29.9 us
    all_to_all x1, waiting for transfers between devices, route(): lax.all_to_all(z.reshape(TILES, OWN * RMAX, 2 * FOCAL), 'tile', 0, 0, til...  22.9 us
    all_to_all x1, starting transfers between devices, route(): lax.all_to_all(z.reshape(TILES, OWN * RMAX, 2 * FOCAL), 'tile', 0, 0, til...  12.1 us
    pallas_call x4, Pallas kernels, window(): pl.pallas_call(window_kernel, in_specs=vmem(GROUPS + 3), out_specs=vmem(G...  10.4 us
    unnamed x24, local copies, waits for them, and re-layouts  7.67 us
    pallas_call x4, Pallas kernels, project(): pl.pallas_call(functools.partial(project_kernel, forward, direct is not N...  6.03 us
  transfers between devices with their start and end apart: 25, of which 23 were waited for; matrix products, arithmetic and copies ran while one was open for 2% of the time, Pallas kernels for 0%

commit v1 on v0

--- a/solution.py
+++ b/solution.py
@@ -20,7 +20,7 @@
 OWN = FREQS // GROUPS
 PW = 8
 SETS = FOCAL // GROUPS // PW
-VMEM_LIMIT = 48 * 1024 * 1024
+VMEM_LIMIT = 24 * 1024 * 1024
 BF = jnp.bfloat16
 F32 = jnp.float32
 
@@ -43,19 +43,17 @@
     return pl.multiple_of(((m + GROUPS - r) % GROUPS * SETS + g) * PW, PW)
 
 
-def project_kernel(forward, use_direct, use_field, *refs):
+def project_kernel(forward, use_field, m_ref, *refs):
     refs = list(refs)
     o_ref = refs.pop()
-    f_ref = refs.pop()
-    if use_direct:
-        m_ref, d_ref = refs[:2]
-        refs = refs[2:]
+    d_ref = refs.pop(0) if forward else None
+    f_ref = refs.pop(0)
     for f in range(OWN):
         plain, turned = [], []
         for r in range(GROUPS):
             for g in range(SETS):
                 real = imag = None
-                if use_direct:
+                if forward:
                     at = pl.ds(focal_start(m_ref[0], r, g), PW)
                     real, imag = d_ref[f, 0, at, :], d_ref[f, 1, at, :]
                 if use_field:
@@ -77,23 +75,39 @@
     return [pl.BlockSpec(memory_space=pltpu.VMEM)] * count
 
 
-def project(forward, factors, direct=None, me=None, field=None):
-    ins, specs = [], []
-    if direct is not None:
-        ins += [me, direct]
-        specs += [pl.BlockSpec(memory_space=pltpu.SMEM)] + vmem()
-    if field is not None:
-        ins += list(field)
-        specs += vmem(GROUPS)
-    return pl.pallas_call(
-        functools.partial(project_kernel, forward, direct is not None, field is not None),
-        in_specs=specs + vmem(),
+def project(me, factors, field=(), direct=None):
+    forward = direct is not None
+    ins = ([direct] if forward else []) + [factors] + list(field)
+    return pl.pallas_call(
+        functools.partial(project_kernel, forward, len(field) > 0),
+        in_specs=[pl.BlockSpec(memory_space=pltpu.SMEM)] + vmem(len(ins)),
         out_specs=vmem()[0],
         out_shape=jax.ShapeDtypeStruct((TILES, OWN, RMAX, 2 * FOCAL), BF),
         compiler_params=params(),
         cost_estimate=pl.CostEstimate(flops=600_000_000, bytes_accessed=5_000_000, transcendentals=0),
         name="project",
-    )(*ins, factors)
+    )(me, *ins)
+
+
+def mask_kernel(mask_ref, f_ref, o_ref):
+    for f in range(OWN):
+        mask = jnp.concatenate([mask_ref[:, f]] * (TILE // 128), axis=2)
+        for c in range(2):
+            o_ref[f, 0, :, c] = f_ref[f, 0, :, c] * mask
+
+
+def masked(factors, tile_ranks):
+    rank = tile_ranks.transpose(2, 0, 1)
+    mask = (lax.broadcasted_iota(jnp.int32, (1, 1, RMAX, 128), 2) < rank[..., None]).astype(BF)
+    return pl.pallas_call(
+        mask_kernel,
+        in_specs=vmem(2),
+        out_specs=vmem()[0],
+        out_shape=jax.ShapeDtypeStruct(factors.shape, BF),
+        compiler_params=params(),
+        cost_estimate=pl.CostEstimate(flops=2_000_000, bytes_accessed=9_000_000, transcendentals=0),
+        name="masked",
+    )(mask, factors)
 
 
 def expand_kernel(forward, z_ref, f_ref, *outs):
@@ -124,28 +138,48 @@
 
 
 def window_kernel(s0, s1, s2, s3, onset_ref, t_ref, f_ref, *outs):
+    half = PW // 2
     rows = OWN * 2 * PW
     count = GROUPS * rows
     lane = lax.broadcasted_iota(jnp.int32, (1, count), 1) % PW
     row = lax.broadcasted_iota(jnp.int32, (count, 1), 0) % PW
+    first = lax.broadcasted_iota(jnp.int32, (count, TILE), 0) % PW < half
     moment = lax.broadcasted_iota(jnp.int32, (SAMPLES, TILE), 0)
-    fields = [
-        jnp.concatenate([ref[:, g].reshape(rows, TILE) for ref in (s0, s1, s2, s3)], axis=0)
-        for g in range(SETS)
-    ]
-    totals = [jnp.zeros((count, TILE), F32) for _ in range(SETS)]
-    for p in range(PW):
-        pick_lane = (lane == p).astype(F32).astype(BF)
-        pick_row = (row == p).astype(F32).astype(BF)
-        inverse = [t_ref[part] * pick_lane for part in range(2)]
-        forward = [f_ref[part] * pick_row for part in range(2)]
-        for g in range(SETS):
-            trace = sum(jnp.dot(part, fields[g], preferred_element_type=F32) for part in inverse)
-            limit = onset_ref[g * PW + p : g * PW + p + 1, :]
-            kept = jnp.where(moment < limit, trace, 0.0).astype(BF)
-            totals[g] += sum(jnp.dot(part, kept, preferred_element_type=F32) for part in forward)
+
+    def one(flags):
+        return flags.astype(F32).astype(BF)
+
+    inverse, forward = [], []
+    for part in range(2):
+        points = [(p, (p + half) % PW) for p in range(part * half, (part + 1) * half)]
+        inverse.append(
+            jnp.concatenate([t_ref[0] * one(lane == p) + t_ref[1] * one(lane == o) for p, o in points], axis=0)
+        )
+        forward.append(
+            jnp.concatenate([f_ref[0] * one(row == p) + f_ref[1] * one(row == o) for p, o in points], axis=1)
+        )
     for g in range(SETS):
-        result = totals[g].astype(BF)
+        whole = jnp.concatenate(
+            [ref[:, g].reshape(rows, TILE) for ref in (s0, s1, s2, s3)], axis=0
+        ).astype(F32)
+        down = pltpu.roll(whole, half, 0)
+        up = pltpu.roll(whole, count - half, 0)
+        fields = [jnp.where(first, whole, down).astype(BF), jnp.where(first, up, whole).astype(BF)]
+        totals = []
+        for part in range(2):
+            trace = jnp.dot(inverse[part], fields[part], preferred_element_type=F32)
+            kept = []
+            for p in range(half):
+                at = g * PW + part * half + p
+                piece = trace[p * SAMPLES : (p + 1) * SAMPLES]
+                kept.append(jnp.where(moment < onset_ref[at : at + 1, :], piece, 0.0).astype(BF))
+            totals.append(
+                jnp.dot(forward[part], jnp.concatenate(kept, axis=0), preferred_element_type=F32)
+            )
+        early, late = totals
+        result = jnp.where(
+            first, early + pltpu.roll(early, count - half, 0), late + pltpu.roll(late, half, 0)
+        ).astype(BF)
         for r in range(GROUPS):
             outs[-r % GROUPS][:, g] = result[r * rows : (r + 1) * rows].reshape(OWN, 2 * PW, TILE)
 
@@ -157,7 +191,7 @@
         out_specs=vmem(GROUPS),
         out_shape=[jax.ShapeDtypeStruct(FIELD, BF)] * GROUPS,
         compiler_params=params(),
-        cost_estimate=pl.CostEstimate(flops=2_200_000_000, bytes_accessed=1_000_000, transcendentals=0),
+        cost_estimate=pl.CostEstimate(flops=1_100_000_000, bytes_accessed=1_000_000, transcendentals=0),
         name="window",
     )(*field, onset, *tables)
 
@@ -240,15 +274,14 @@
     index = me.reshape(1).astype(jnp.int32)
     tables = own_tables(me)
     sources, receivers = own_onsets(onsets_source, me), own_onsets(onsets_receiver, me)
-    inside = lax.broadcasted_iota(jnp.int32, (1, 1, 1, 1, RMAX, 1), 4)
-    u_own = u_factors * (inside < tile_ranks[:, :, :, None, None, None]).astype(BF)
-
-    plus = None
+    u_own = masked(u_factors, tile_ranks)
+
+    plus = ()
     for _ in range(ITERS):
-        z = project(True, v_factors, direct_field, index, plus)
+        z = project(index, v_factors, plus, direct_field)
         image = exchange(expand(True, route(z), u_own))
         minus = exchange(window(image, sources, tables))
-        w = project(False, u_own, field=minus)
+        w = project(index, u_own, minus)
         image = exchange(expand(False, route(w), v_factors))
         plus = exchange(window(image, receivers, tables))
     return (finish(index, plus, direct_field), finish(index, minus))

time: 251 us -> 231 us (0.920); the launches traced: 247 us -> 231 us
  starting transfers between devices: 57.7 us -> 48.8 us
  other arithmetic: 4.01 us -> 0.34 us
  Pallas kernels: 21 us -> 17.4 us
    ppermute x24, starting transfers between devices: 45.6 us -> 36.6 us  [exchange(): lax.ppermute(parts[r], 'freq', [(i, (i + r) % GROUPS) for i in range(GROU...]
    pallas_call x4, Pallas kernels: 10.4 us -> 6.22 us  [window(): pl.pallas_call(window_kernel, in_specs=vmem(GROUPS + 3), out_specs=vmem(G...]
    mul x1 -> x0, other arithmetic: 3.91 us -> none  [per_device(): u_factors * (inside < tile_ranks[:, :, :, None, None, None]).astype(BF)]
    pallas_call x4 -> x5, Pallas kernels: 6.03 us -> 6.46 us  [the longest x4 6.02 us: project(): pl.pallas_call(functools.partial(project_kernel, forward, len(field) > 0)...]
  transfers between devices with their start and end apart: 25 -> 25, of which waited for: 23 -> 25; matrix products, arithmetic and copies ran while one was open for 2% -> 1% of each run, Pallas kernels for 0% -> 1%
where the time goes in v1:
time: 231 us
  blocking collectives  100 us (43%)
  waiting for transfers between devices  52.4 us (23%)
  starting transfers between devices  48.8 us (21%)
  Pallas kernels  17.4 us (8%)
  local copies, waits for them, and re-layouts  10.6 us (5%)
    all_to_all x3, blocking collectives, route(): lax.all_to_all(z.reshape(TILES, OWN * RMAX, 2 * FOCAL), 'tile', 0, 0, til...  100 us
    ppermute x24, starting transfers between devices, exchange(): lax.ppermute(parts[r], 'freq', [(i, (i + r) % GROUPS) for i in range(GROU...  36.6 us
    ppermute x24, waiting for transfers between devices, exchange(): lax.ppermute(parts[r], 'freq', [(i, (i + r) % GROUPS) for i in range(GROU...  30.5 us
    all_to_all x1, waiting for transfers between devices, route(): lax.all_to_all(z.reshape(TILES, OWN * RMAX, 2 * FOCAL), 'tile', 0, 0, til...  21.9 us
    all_to_all x1, starting transfers between devices, route(): lax.all_to_all(z.reshape(TILES, OWN * RMAX, 2 * FOCAL), 'tile', 0, 0, til...  12.1 us
    unnamed x24, local copies, waits for them, and re-layouts  9.61 us
    pallas_call x4, Pallas kernels, window(): pl.pallas_call(window_kernel, in_specs=vmem(GROUPS + 3), out_specs=vmem(G...  6.22 us
    pallas_call x4, Pallas kernels, project(): pl.pallas_call(functools.partial(project_kernel, forward, len(field) > 0)...  6.02 us
  transfers between devices with their start and end apart: 25, of which 25 were waited for; matrix products, arithmetic and copies ran while one was open for 1% of the time, Pallas kernels for 1%

profile of v1, /device:TPU:8, one launch (start us, length us, event | category | flops | bytes accessed | tf_op | source)
XLA Modules:
  0.0 230.8 jit_solution(8064274271313919773)
XLA Ops:
  0.7 2.2 copy-done.4
  3.9 2.3 project.4
  6.2 12.1 %all-to-all-start = ((bf16[64,64,128]{2,1,0:T(8,128)(2,1)}), bf16[64,64,128]{2,1,0:T(8,128)(2,1)S(1)}, u32[]{:S(2)}, u32[]{:S(2)}) async-start(bf16[64,64,128]{2,1,0:T(8,128)(2,1)} %bitcast.3), calls=%async_computation | async-start | bytes 2097152 | tf_op jit(solution)/shard_map/all_to_all | solution.py:267
  18.8 2.2 copy-done.8
  21.4 1.9 copy-done.1
  23.5 21.9 %all-to-all-done = bf16[64,64,128]{2,1,0:T(8,128)(2,1)S(1)} async-done(((bf16[64,64,128]{2,1,0:T(8,128)(2,1)}), bf16[64,64,128]{2,1,0:T(8,128)(2,1)S(1)}, u32[]{:S(2)}, u32[]{:S(2)}) %all-to-all-start) | async-done | bytes 1048608 | tf_op jit(solution)/shard_map/all_to_all | solution.py:267
  45.4 2.2 copy-done.2
  48.4 1.6 collective-permute-start
  49.9 2.7 %collective-permute-start.1 = (bf16[4,2,16,256]{3,2,1,0:T(8,128)(2,1)S(1)}, bf16[4,2,16,256]{3,2,1,0:T(8,128)(2,1)S(1)}, u32[]{:S(2)}, u32[]{:S(2)}) collective-permute-start(bf16[4,2,16,256]{3,2,1,0:T(8,128)(2,1)S(1)} %get-tuple-element.36), channel_id=1, source_target_pairs={{0,128},{64,192},{128,0},{192,64},{1,129},{65,193},{129,1},{193,65... | collective-permute-start | bytes 196616 | tf_op jit(solution)/shard_map/ppermute | solution.py:256
  52.7 1.4 collective-permute-start.2
  54.3 2.4 %collective-permute-done.1.s2 = bf16[4,2,16,256]{3,2,1,0:T(8,128)(2,1)S(1)} collective-permute-done((bf16[4,2,16,256]{3,2,1,0:T(8,128)(2,1)S(1)}, bf16[4,2,16,256]{3,2,1,0:T(8,128)(2,1)S(1)}, u32[]{:S(2)}, u32[]{:S(2)}) %collective-permute-start.1) | collective-permute-done | bytes 65568 | tf_op jit(solution)/shard_map/ppermute | solution.py:256
  57.5 1.6 window.4
  59.1 1.4 collective-permute-start.3
  60.5 2.8 %collective-permute-start.4 = (bf16[4,2,16,256]{3,2,1,0:T(8,128)(2,1)S(1)}, bf16[4,2,16,256]{3,2,1,0:T(8,128)(2,1)S(1)}, u32[]{:S(2)}, u32[]{:S(2)}) collective-permute-start(bf16[4,2,16,256]{3,2,1,0:T(8,128)(2,1)S(1)} %get-tuple-element.40), channel_id=1, source_target_pairs={{0,128},{64,192},{128,0},{192,64},{1,129},{65,193},{129,1},{193,65... | collective-permute-start | bytes 196616 | tf_op jit(solution)/shard_map/ppermute | solution.py:256
  65.0 1.6 collective-permute-done.4.refs_3_
  67.5 1.2 project.5
  68.8 34.0 %all_to_all.20 = bf16[64,64,128]{2,1,0:T(8,128)(2,1)S(1)} all-to-all(bf16[64,64,128]{2,1,0:T(8,128)(2,1)S(1)} %bitcast.16), channel_id=1, replica_groups=mesh['freq'=4,'tile'=64] {'tile'}, dimensions={0} | all-to-all | bytes 2097152 | tf_op jit(solution)/shard_map/all_to_all | solution.py:267
  103.8 2.9 %collective-permute-start.7 = (bf16[4,2,16,256]{3,2,1,0:T(8,128)(2,1)S(1)}, bf16[4,2,16,256]{3,2,1,0:T(8,128)(2,1)S(1)}, u32[]{:S(2)}, u32[]{:S(2)}) collective-permute-start(bf16[4,2,16,256]{3,2,1,0:T(8,128)(2,1)S(1)} %get-tuple-element.44), channel_id=1, source_target_pairs={{0,128},{64,192},{128,0},{192,64},{1,129},{65,193},{129,1},{193,65... | collective-permute-start | bytes 196616 | tf_op jit(solution)/shard_map/ppermute | solution.py:256
  106.7 1.2 collective-permute-start.8
  108.7 1.3 collective-permute-done.6.s1
  110.8 1.3 collective-permute-done.8.s3
  112.1 1.6 window.5
  113.6 1.1 collective-permute-start.9
  114.8 3.2 %collective-permute-start.10 = (bf16[4,2,16,256]{3,2,1,0:T(8,128)(2,1)S(1)}, bf16[4,2,16,256]{3,2,1,0:T(8,128)(2,1)S(1)}, u32[]{:S(2)}, u32[]{:S(2)}) collective-permute-start(bf16[4,2,16,256]{3,2,1,0:T(8,128)(2,1)S(1)} %get-tuple-element.48), channel_id=1, source_target_pairs={{0,128},{64,192},{128,0},{192,64},{1,129},{65,193},{129,1},{193,65... | collective-permute-start | bytes 196616 | tf_op jit(solution)/shard_map/ppermute | solution.py:256
  118.0 1.2 collective-permute-done.9.refs_3_
  119.2 2.3 collective-permute-done.10.refs_4_
  122.3 1.3 project.6
  123.5 33.2 %all_to_all.21 = bf16[64,64,128]{2,1,0:T(8,128)(2,1)S(1)} all-to-all(bf16[64,64,128]{2,1,0:T(8,128)(2,1)S(1)} %bitcast.17), channel_id=1, replica_groups=mesh['freq'=4,'tile'=64] {'tile'}, dimensions={0} | all-to-all | bytes 2097152 | tf_op jit(solution)/shard_map/all_to_all | solution.py:267
  157.6 2.9 %collective-permute-start.13 = (bf16[4,2,16,256]{3,2,1,0:T(8,128)(2,1)S(1)}, bf16[4,2,16,256]{3,2,1,0:T(8,128)(2,1)S(1)}, u32[]{:S(2)}, u32[]{:S(2)}) collective-permute-start(bf16[4,2,16,256]{3,2,1,0:T(8,128)(2,1)S(1)} %get-tuple-element.52), channel_id=1, source_target_pairs={{0,128},{64,192},{128,0},{192,64},{1,129},{65,193},{129,1},{193,65... | collective-permute-start | bytes 196616 | tf_op jit(solution)/shard_map/ppermute | solution.py:256
  160.5 1.3 collective-permute-start.14
  161.8 2.0 collective-permute-done.12.s1
  164.6 1.3 collective-permute-done.14.s3
  165.9 1.6 window.6
  167.5 1.1 collective-permute-start.15
  168.6 3.2 %collective-permute-start.16 = (bf16[4,2,16,256]{3,2,1,0:T(8,128)(2,1)S(1)}, bf16[4,2,16,256]{3,2,1,0:T(8,128)(2,1)S(1)}, u32[]{:S(2)}, u32[]{:S(2)}) collective-permute-start(bf16[4,2,16,256]{3,2,1,0:T(8,128)(2,1)S(1)} %get-tuple-element.56), channel_id=1, source_target_pairs={{0,128},{64,192},{128,0},{192,64},{1,129},{65,193},{129,1},{193,65... | collective-permute-start | bytes 196616 | tf_op jit(solution)/shard_map/ppermute | solution.py:256
  171.8 1.2 collective-permute-done.15.refs_2_
  173.0 2.3 collective-permute-done.16.refs_3_
  176.1 1.2 project.7
  177.4 33.2 %all_to_all.22 = bf16[64,64,128]{2,1,0:T(8,128)(2,1)S(1)} all-to-all(bf16[64,64,128]{2,1,0:T(8,128)(2,1)S(1)} %bitcast.18), channel_id=1, replica_groups=mesh['freq'=4,'tile'=64] {'tile'}, dimensions={0} | all-to-all | bytes 2097152 | tf_op jit(solution)/shard_map/all_to_all | solution.py:267
  211.5 3.0 %collective-permute-start.19 = (bf16[4,2,16,256]{3,2,1,0:T(8,128)(2,1)S(1)}, bf16[4,2,16,256]{3,2,1,0:T(8,128)(2,1)S(1)}, u32[]{:S(2)}, u32[]{:S(2)}) collective-permute-start(bf16[4,2,16,256]{3,2,1,0:T(8,128)(2,1)S(1)} %get-tuple-element.60), channel_id=1, source_target_pairs={{0,128},{64,192},{128,0},{192,64},{1,129},{65,193},{129,1},{193,65... | collective-permute-start | bytes 196616 | tf_op jit(solution)/shard_map/ppermute | solution.py:256
  214.5 1.1 collective-permute-start.20
  215.6 1.9 collective-permute-done.18.s1
  217.5 1.1 collective-permute-done.19.s2
  218.5 1.2 collective-permute-done.20.s3
  219.7 1.6 window.7
  221.3 1.1 collective-permute-start.21
  222.4 3.2 %collective-permute-start.22 = (bf16[4,2,16,256]{3,2,1,0:T(8,128)(2,1)S(1)}, bf16[4,2,16,256]{3,2,1,0:T(8,128)(2,1)S(1)}, u32[]{:S(2)}, u32[]{:S(2)}) collective-permute-start(bf16[4,2,16,256]{3,2,1,0:T(8,128)(2,1)S(1)} %get-tuple-element.64), channel_id=1, source_target_pairs={{0,128},{64,192},{128,0},{192,64},{1,129},{65,193},{129,1},{193,65... | collective-permute-start | bytes 196616 | tf_op jit(solution)/shard_map/ppermute | solution.py:256
  226.8 2.3 collective-permute-done.22.refs_4_
  (49 shorter events, 15.9 us)
Async XLA Ops:
  0.6 53.5 %copy-start = (s32[64,256]{1,0:T(8,128)S(1)}, s32[64,256]{1,0:T(8,128)}, u32[]{:S(2)}) copy-start(s32[64,256]{1,0:T(8,128)} %param.12) | copy-start | bytes 196612
  0.6 17.7 %copy-start.11 = (s32[4,1,64]{2,1,0:T(1,128)S(1)}, s32[4,1,64]{2,1,0:T(1,128)}, u32[]{:S(2)}) copy-start(s32[4,1,64]{2,1,0:T(1,128)} %param.11) | copy-start | bytes 3076
  0.7 2.2 copy-start.4
  2.9 1.0 copy-start.6
  6.2 39.2 %all-to-all-start = ((bf16[64,64,128]{2,1,0:T(8,128)(2,1)}), bf16[64,64,128]{2,1,0:T(8,128)(2,1)S(1)}, u32[]{:S(2)}, u32[]{:S(2)}) async-start(bf16[64,64,128]{2,1,0:T(8,128)(2,1)} %bitcast.3), calls=%async_computation | async-start | bytes 2097152 | tf_op jit(solution)/shard_map/all_to_all | solution.py:267
  18.8 2.2 copy-start.8
  21.0 2.4 %copy-start.9 = (bf16[2,448,256]{2,1,0:T(8,128)(2,1)S(1)}, bf16[2,448,256]{2,1,0:T(8,128)(2,1)}, u32[]{:S(2)}) copy-start(bf16[2,448,256]{2,1,0:T(8,128)(2,1)} %constant.21.clone) | copy-start | bytes 1376260
  21.0 2.4 %copy-start.10 = (bf16[2,256,448]{2,1,0:T(8,128)(2,1)S(1)}, bf16[2,256,448]{2,1,0:T(8,128)(2,1)}, u32[]{:S(2)}) copy-start(bf16[2,256,448]{2,1,0:T(8,128)(2,1)} %constant.20.clone) | copy-start | bytes 1376260
  21.4 2.0 copy-start.1
  45.4 2.2 copy-start.2
  47.6 19.9 %copy-start.3 = (bf16[4,1,64,2,16,256]{5,4,3,2,1,0:T(8,128)(2,1)S(1)}, bf16[4,1,64,2,16,256]{5,4,3,2,1,0:T(8,128)(2,1)}, u32[]{:S(2)}) copy-start(bf16[4,1,64,2,16,256]{5,4,3,2,1,0:T(8,128)(2,1)} %copy-done.1) | copy-start | bytes 12582916
  48.4 5.9 %collective-permute-start = (bf16[4,2,16,256]{3,2,1,0:T(8,128)(2,1)S(1)}, bf16[4,2,16,256]{3,2,1,0:T(8,128)(2,1)S(1)}, u32[]{:S(2)}, u32[]{:S(2)}) collective-permute-start(bf16[4,2,16,256]{3,2,1,0:T(8,128)(2,1)S(1)} %get-tuple-element.35), channel_id=1, source_target_pairs={{0,64},{64,128},{128,192},{192,0},{1,65},{65,129},{129,193},{193,1... | collective-permute-start | bytes 196616 | tf_op jit(solution)/shard_map/ppermute | solution.py:256
  49.9 6.7 %collective-permute-start.1 = (bf16[4,2,16,256]{3,2,1,0:T(8,128)(2,1)S(1)}, bf16[4,2,16,256]{3,2,1,0:T(8,128)(2,1)S(1)}, u32[]{:S(2)}, u32[]{:S(2)}) collective-permute-start(bf16[4,2,16,256]{3,2,1,0:T(8,128)(2,1)S(1)} %get-tuple-element.36), channel_id=1, source_target_pairs={{0,128},{64,192},{128,0},{192,64},{1,129},{65,193},{129,1},{193,65... | collective-permute-start | bytes 196616 | tf_op jit(solution)/shard_map/ppermute | solution.py:256
  52.7 4.8 %collective-permute-start.2 = (bf16[4,2,16,256]{3,2,1,0:T(8,128)(2,1)S(1)}, bf16[4,2,16,256]{3,2,1,0:T(8,128)(2,1)S(1)}, u32[]{:S(2)}, u32[]{:S(2)}) collective-permute-start(bf16[4,2,16,256]{3,2,1,0:T(8,128)(2,1)S(1)} %get-tuple-element.37), channel_id=1, source_target_pairs={{0,192},{64,0},{128,64},{192,128},{1,193},{65,1},{129,65},{193,129... | collective-permute-start | bytes 196616 | tf_op jit(solution)/shard_map/ppermute | solution.py:256
  59.1 43.7 %copy-start.5 = (bf16[4,64,1,2,16,256]{5,4,3,2,1,0:T(8,128)(2,1)S(1)}, bf16[4,64,1,2,16,256]{5,4,3,2,1,0:T(8,128)(2,1)}, u32[]{:S(2)}) copy-start(bf16[4,64,1,2,16,256]{5,4,3,2,1,0:T(8,128)(2,1)} %f_ref.5) | copy-start | bytes 12582916
  59.1 5.9 %collective-permute-start.3 = (bf16[4,2,16,256]{3,2,1,0:T(8,128)(2,1)S(1)}, bf16[4,2,16,256]{3,2,1,0:T(8,128)(2,1)S(1)}, u32[]{:S(2)}, u32[]{:S(2)}) collective-permute-start(bf16[4,2,16,256]{3,2,1,0:T(8,128)(2,1)S(1)} %get-tuple-element.39), channel_id=1, source_target_pairs={{0,64},{64,128},{128,192},{192,0},{1,65},{65,129},{129,193},{193,1... | collective-permute-start | bytes 196616 | tf_op jit(solution)/shard_map/ppermute | solution.py:256
  60.5 6.2 %collective-permute-start.4 = (bf16[4,2,16,256]{3,2,1,0:T(8,128)(2,1)S(1)}, bf16[4,2,16,256]{3,2,1,0:T(8,128)(2,1)S(1)}, u32[]{:S(2)}, u32[]{:S(2)}) collective-permute-start(bf16[4,2,16,256]{3,2,1,0:T(8,128)(2,1)S(1)} %get-tuple-element.40), channel_id=1, source_target_pairs={{0,128},{64,192},{128,0},{192,64},{1,129},{65,193},{129,1},{193,65... | collective-permute-start | bytes 196616 | tf_op jit(solution)/shard_map/ppermute | solution.py:256
  63.3 4.3 %collective-permute-start.5 = (bf16[4,2,16,256]{3,2,1,0:T(8,128)(2,1)S(1)}, bf16[4,2,16,256]{3,2,1,0:T(8,128)(2,1)S(1)}, u32[]{:S(2)}, u32[]{:S(2)}) collective-permute-start(bf16[4,2,16,256]{3,2,1,0:T(8,128)(2,1)S(1)} %get-tuple-element.41), channel_id=1, source_target_pairs={{0,192},{64,0},{128,64},{192,128},{1,193},{65,1},{129,65},{193,129... | collective-permute-start | bytes 196616 | tf_op jit(solution)/shard_map/ppermute | solution.py:256
  102.8 19.5 %copy-start.7 = (f32[4,2,64,256]{3,2,1,0:T(8,128)S(1)}, f32[4,2,64,256]{3,2,1,0:T(8,128)}, u32[]{:S(2)}) copy-start(f32[4,2,64,256]{3,2,1,0:T(8,128)} %refs_1_.5) | copy-start | bytes 1572868
  103.5 6.4 %collective-permute-start.6 = (bf16[4,2,16,256]{3,2,1,0:T(8,128)(2,1)S(1)}, bf16[4,2,16,256]{3,2,1,0:T(8,128)(2,1)S(1)}, u32[]{:S(2)}, u32[]{:S(2)}) collective-permute-start(bf16[4,2,16,256]{3,2,1,0:T(8,128)(2,1)S(1)} %get-tuple-element.43), channel_id=1, source_target_pairs={{0,64},{64,128},{128,192},{192,0},{1,65},{65,129},{129,193},{193,1... | collective-permute-start | bytes 196616 | tf_op jit(solution)/shard_map/ppermute | solution.py:256
  103.8 7.0 %collective-permute-start.7 = (bf16[4,2,16,256]{3,2,1,0:T(8,128)(2,1)S(1)}, bf16[4,2,16,256]{3,2,1,0:T(8,128)(2,1)S(1)}, u32[]{:S(2)}, u32[]{:S(2)}) collective-permute-start(bf16[4,2,16,256]{3,2,1,0:T(8,128)(2,1)S(1)} %get-tuple-element.44), channel_id=1, source_target_pairs={{0,128},{64,192},{128,0},{192,64},{1,129},{65,193},{129,1},{193,65... | collective-permute-start | bytes 196616 | tf_op jit(solution)/shard_map/ppermute | solution.py:256
  106.7 5.4 %collective-permute-start.8 = (bf16[4,2,16,256]{3,2,1,0:T(8,128)(2,1)S(1)}, bf16[4,2,16,256]{3,2,1,0:T(8,128)(2,1)S(1)}, u32[]{:S(2)}, u32[]{:S(2)}) collective-permute-start(bf16[4,2,16,256]{3,2,1,0:T(8,128)(2,1)S(1)} %get-tuple-element.45), channel_id=1, source_target_pairs={{0,192},{64,0},{128,64},{192,128},{1,193},{65,1},{129,65},{193,129... | collective-permute-start | bytes 196616 | tf_op jit(solution)/shard_map/ppermute | solution.py:256
  113.6 5.6 %collective-permute-start.9 = (bf16[4,2,16,256]{3,2,1,0:T(8,128)(2,1)S(1)}, bf16[4,2,16,256]{3,2,1,0:T(8,128)(2,1)S(1)}, u32[]{:S(2)}, u32[]{:S(2)}) collective-permute-start(bf16[4,2,16,256]{3,2,1,0:T(8,128)(2,1)S(1)} %get-tuple-element.47), channel_id=1, source_target_pairs={{0,64},{64,128},{128,192},{192,0},{1,65},{65,129},{129,193},{193,1... | collective-permute-start | bytes 196616 | tf_op jit(solution)/shard_map/ppermute | solution.py:256
  114.8 6.7 %collective-permute-start.10 = (bf16[4,2,16,256]{3,2,1,0:T(8,128)(2,1)S(1)}, bf16[4,2,16,256]{3,2,1,0:T(8,128)(2,1)S(1)}, u32[]{:S(2)}, u32[]{:S(2)}) collective-permute-start(bf16[4,2,16,256]{3,2,1,0:T(8,128)(2,1)S(1)} %get-tuple-element.48), channel_id=1, source_target_pairs={{0,128},{64,192},{128,0},{192,64},{1,129},{65,193},{129,1},{193,65... | collective-permute-start | bytes 196616 | tf_op jit(solution)/shard_map/ppermute | solution.py:256
  118.0 4.3 %collective-permute-start.11 = (bf16[4,2,16,256]{3,2,1,0:T(8,128)(2,1)S(1)}, bf16[4,2,16,256]{3,2,1,0:T(8,128)(2,1)S(1)}, u32[]{:S(2)}, u32[]{:S(2)}) collective-permute-start(bf16[4,2,16,256]{3,2,1,0:T(8,128)(2,1)S(1)} %get-tuple-element.49), channel_id=1, source_target_pairs={{0,192},{64,0},{128,64},{192,128},{1,193},{65,1},{129,65},{193,129... | collective-permute-start | bytes 196616 | tf_op jit(solution)/shard_map/ppermute | solution.py:256
  157.5 6.2 %collective-permute-start.12 = (bf16[4,2,16,256]{3,2,1,0:T(8,128)(2,1)S(1)}, bf16[4,2,16,256]{3,2,1,0:T(8,128)(2,1)S(1)}, u32[]{:S(2)}, u32[]{:S(2)}) collective-permute-start(bf16[4,2,16,256]{3,2,1,0:T(8,128)(2,1)S(1)} %get-tuple-element.51), channel_id=1, source_target_pairs={{0,64},{64,128},{128,192},{192,0},{1,65},{65,129},{129,193},{193,1... | collective-permute-start | bytes 196616 | tf_op jit(solution)/shard_map/ppermute | solution.py:256
  157.6 7.0 %collective-permute-start.13 = (bf16[4,2,16,256]{3,2,1,0:T(8,128)(2,1)S(1)}, bf16[4,2,16,256]{3,2,1,0:T(8,128)(2,1)S(1)}, u32[]{:S(2)}, u32[]{:S(2)}) collective-permute-start(bf16[4,2,16,256]{3,2,1,0:T(8,128)(2,1)S(1)} %get-tuple-element.52), channel_id=1, source_target_pairs={{0,128},{64,192},{128,0},{192,64},{1,129},{65,193},{129,1},{193,65... | collective-permute-start | bytes 196616 | tf_op jit(solution)/shard_map/ppermute | solution.py:256
  160.5 5.4 %collective-permute-start.14 = (bf16[4,2,16,256]{3,2,1,0:T(8,128)(2,1)S(1)}, bf16[4,2,16,256]{3,2,1,0:T(8,128)(2,1)S(1)}, u32[]{:S(2)}, u32[]{:S(2)}) collective-permute-start(bf16[4,2,16,256]{3,2,1,0:T(8,128)(2,1)S(1)} %get-tuple-element.53), channel_id=1, source_target_pairs={{0,192},{64,0},{128,64},{192,128},{1,193},{65,1},{129,65},{193,129... | collective-permute-start | bytes 196616 | tf_op jit(solution)/shard_map/ppermute | solution.py:256
  167.5 5.6 %collective-permute-start.15 = (bf16[4,2,16,256]{3,2,1,0:T(8,128)(2,1)S(1)}, bf16[4,2,16,256]{3,2,1,0:T(8,128)(2,1)S(1)}, u32[]{:S(2)}, u32[]{:S(2)}) collective-permute-start(bf16[4,2,16,256]{3,2,1,0:T(8,128)(2,1)S(1)} %get-tuple-element.55), channel_id=1, source_target_pairs={{0,64},{64,128},{128,192},{192,0},{1,65},{65,129},{129,193},{193,1... | collective-permute-start | bytes 196616 | tf_op jit(solution)/shard_map/ppermute | solution.py:256
  168.6 6.7 %collective-permute-start.16 = (bf16[4,2,16,256]{3,2,1,0:T(8,128)(2,1)S(1)}, bf16[4,2,16,256]{3,2,1,0:T(8,128)(2,1)S(1)}, u32[]{:S(2)}, u32[]{:S(2)}) collective-permute-start(bf16[4,2,16,256]{3,2,1,0:T(8,128)(2,1)S(1)} %get-tuple-element.56), channel_id=1, source_target_pairs={{0,128},{64,192},{128,0},{192,64},{1,129},{65,193},{129,1},{193,65... | collective-permute-start | bytes 196616 | tf_op jit(solution)/shard_map/ppermute | solution.py:256
  171.8 4.3 %collective-permute-start.17 = (bf16[4,2,16,256]{3,2,1,0:T(8,128)(2,1)S(1)}, bf16[4,2,16,256]{3,2,1,0:T(8,128)(2,1)S(1)}, u32[]{:S(2)}, u32[]{:S(2)}) collective-permute-start(bf16[4,2,16,256]{3,2,1,0:T(8,128)(2,1)S(1)} %get-tuple-element.57), channel_id=1, source_target_pairs={{0,192},{64,0},{128,64},{192,128},{1,193},{65,1},{129,65},{193,129... | collective-permute-start | bytes 196616 | tf_op jit(solution)/shard_map/ppermute | solution.py:256
  211.4 6.1 %collective-permute-start.18 = (bf16[4,2,16,256]{3,2,1,0:T(8,128)(2,1)S(1)}, bf16[4,2,16,256]{3,2,1,0:T(8,128)(2,1)S(1)}, u32[]{:S(2)}, u32[]{:S(2)}) collective-permute-start(bf16[4,2,16,256]{3,2,1,0:T(8,128)(2,1)S(1)} %get-tuple-element.59), channel_id=1, source_target_pairs={{0,64},{64,128},{128,192},{192,0},{1,65},{65,129},{129,193},{193,1... | collective-permute-start | bytes 196616 | tf_op jit(solution)/shard_map/ppermute | solution.py:256
  211.5 7.1 %collective-permute-start.19 = (bf16[4,2,16,256]{3,2,1,0:T(8,128)(2,1)S(1)}, bf16[4,2,16,256]{3,2,1,0:T(8,128)(2,1)S(1)}, u32[]{:S(2)}, u32[]{:S(2)}) collective-permute-start(bf16[4,2,16,256]{3,2,1,0:T(8,128)(2,1)S(1)} %get-tuple-element.60), channel_id=1, source_target_pairs={{0,128},{64,192},{128,0},{192,64},{1,129},{65,193},{129,1},{193,65... | collective-permute-start | bytes 196616 | tf_op jit(solution)/shard_map/ppermute | solution.py:256
  214.5 5.3 %collective-permute-start.20 = (bf16[4,2,16,256]{3,2,1,0:T(8,128)(2,1)S(1)}, bf16[4,2,16,256]{3,2,1,0:T(8,128)(2,1)S(1)}, u32[]{:S(2)}, u32[]{:S(2)}) collective-permute-start(bf16[4,2,16,256]{3,2,1,0:T(8,128)(2,1)S(1)} %get-tuple-element.61), channel_id=1, source_target_pairs={{0,192},{64,0},{128,64},{192,128},{1,193},{65,1},{129,65},{193,129... | collective-permute-start | bytes 196616 | tf_op jit(solution)/shard_map/ppermute | solution.py:256
  221.3 5.6 %collective-permute-start.21 = (bf16[4,2,16,256]{3,2,1,0:T(8,128)(2,1)S(1)}, bf16[4,2,16,256]{3,2,1,0:T(8,128)(2,1)S(1)}, u32[]{:S(2)}, u32[]{:S(2)}) collective-permute-start(bf16[4,2,16,256]{3,2,1,0:T(8,128)(2,1)S(1)} %get-tuple-element.63), channel_id=1, source_target_pairs={{0,64},{64,128},{128,192},{192,0},{1,65},{65,129},{129,193},{193,1... | collective-permute-start | bytes 196616 | tf_op jit(solution)/shard_map/ppermute | solution.py:256
  222.4 6.7 %collective-permute-start.22 = (bf16[4,2,16,256]{3,2,1,0:T(8,128)(2,1)S(1)}, bf16[4,2,16,256]{3,2,1,0:T(8,128)(2,1)S(1)}, u32[]{:S(2)}, u32[]{:S(2)}) collective-permute-start(bf16[4,2,16,256]{3,2,1,0:T(8,128)(2,1)S(1)} %get-tuple-element.64), channel_id=1, source_target_pairs={{0,128},{64,192},{128,0},{192,64},{1,129},{65,193},{129,1},{193,65... | collective-permute-start | bytes 196616 | tf_op jit(solution)/shard_map/ppermute | solution.py:256
  225.7 4.3 %collective-permute-start.23 = (bf16[4,2,16,256]{3,2,1,0:T(8,128)(2,1)S(1)}, bf16[4,2,16,256]{3,2,1,0:T(8,128)(2,1)S(1)}, u32[]{:S(2)}, u32[]{:S(2)}) collective-permute-start(bf16[4,2,16,256]{3,2,1,0:T(8,128)(2,1)S(1)} %get-tuple-element.65), channel_id=1, source_target_pairs={{0,192},{64,0},{128,64},{192,128},{1,193},{65,1},{129,65},{193,129... | collective-permute-start | bytes 196616 | tf_op jit(solution)/shard_map/ppermute | solution.py:256

commit v2 on v1

--- a/solution.py
+++ b/solution.py
@@ -44,10 +44,7 @@
 
 
 def project_kernel(forward, use_field, m_ref, *refs):
-    refs = list(refs)
-    o_ref = refs.pop()
-    d_ref = refs.pop(0) if forward else None
-    f_ref = refs.pop(0)
+    d_ref, f_ref, *refs, o_ref = refs
     for f in range(OWN):
         plain, turned = [], []
         for r in range(GROUPS):
@@ -68,51 +65,32 @@
             factor = f_ref[f, :, 0, part] if forward else f_ref[f, 0, :, part]
             term = dot_nt(factor.reshape(TILES * RMAX, TILE), x)
             total = term if total is None else total + term
-        o_ref[:, f] = total.astype(BF).reshape(TILES, RMAX, 2 * FOCAL)
+        z = total.astype(BF).reshape(TILES, RMAX, 2 * FOCAL)
+        o_ref[:, f] = z if forward else z * d_ref[f]
 
 
 def vmem(count=1):
     return [pl.BlockSpec(memory_space=pltpu.VMEM)] * count
 
 
-def project(me, factors, field=(), direct=None):
-    forward = direct is not None
-    ins = ([direct] if forward else []) + [factors] + list(field)
+def project(forward, me, other, factors, field=()):
     return pl.pallas_call(
         functools.partial(project_kernel, forward, len(field) > 0),
-        in_specs=[pl.BlockSpec(memory_space=pltpu.SMEM)] + vmem(len(ins)),
+        in_specs=[pl.BlockSpec(memory_space=pltpu.SMEM)] + vmem(2 + len(field)),
         out_specs=vmem()[0],
         out_shape=jax.ShapeDtypeStruct((TILES, OWN, RMAX, 2 * FOCAL), BF),
         compiler_params=params(),
         cost_estimate=pl.CostEstimate(flops=600_000_000, bytes_accessed=5_000_000, transcendentals=0),
         name="project",
-    )(me, *ins)
-
-
-def mask_kernel(mask_ref, f_ref, o_ref):
+    )(me, other, factors, *field)
+
+
+def expand_kernel(forward, z_ref, f_ref, *outs):
+    if forward:
+        mask_ref, *outs = outs
     for f in range(OWN):
-        mask = jnp.concatenate([mask_ref[:, f]] * (TILE // 128), axis=2)
-        for c in range(2):
-            o_ref[f, 0, :, c] = f_ref[f, 0, :, c] * mask
-
-
-def masked(factors, tile_ranks):
-    rank = tile_ranks.transpose(2, 0, 1)
-    mask = (lax.broadcasted_iota(jnp.int32, (1, 1, RMAX, 128), 2) < rank[..., None]).astype(BF)
-    return pl.pallas_call(
-        mask_kernel,
-        in_specs=vmem(2),
-        out_specs=vmem()[0],
-        out_shape=jax.ShapeDtypeStruct(factors.shape, BF),
-        compiler_params=params(),
-        cost_estimate=pl.CostEstimate(flops=2_000_000, bytes_accessed=9_000_000, transcendentals=0),
-        name="masked",
-    )(mask, factors)
-
-
-def expand_kernel(forward, z_ref, f_ref, *outs):
-    for f in range(OWN):
-        z = z_ref[:, f].reshape(TILES * RMAX, 2 * FOCAL)
+        z = z_ref[:, f] * mask_ref[f] if forward else z_ref[:, f]
+        z = z.reshape(TILES * RMAX, 2 * FOCAL)
         straight, crossed = [
             dot_tn(z, (f_ref[f, 0, :, c] if forward else f_ref[f, :, 0, c]).reshape(TILES * RMAX, TILE))
             for c in range(2)
@@ -125,16 +103,17 @@
                 outs[-r % GROUPS][f, g] = jnp.concatenate([real_part, imag_part], axis=0).astype(BF)
 
 
-def expand(forward, z, factors):
+def expand(forward, z, factors, mask=None):
+    ins = [z, factors] + ([mask] if forward else [])
     return pl.pallas_call(
         functools.partial(expand_kernel, forward),
-        in_specs=vmem(2),
+        in_specs=vmem(len(ins)),
         out_specs=vmem(GROUPS),
         out_shape=[jax.ShapeDtypeStruct(FIELD, BF)] * GROUPS,
         compiler_params=params(),
         cost_estimate=pl.CostEstimate(flops=600_000_000, bytes_accessed=5_000_000, transcendentals=0),
         name="expand",
-    )(z, factors)
+    )(*ins)
 
 
 def window_kernel(s0, s1, s2, s3, onset_ref, t_ref, f_ref, *outs):
@@ -272,16 +251,21 @@
 def per_device(direct_field, u_factors, v_factors, tile_ranks, onsets_source, onsets_receiver):
     me = lax.axis_index("freq")
     index = me.reshape(1).astype(jnp.int32)
-    tables = own_tables(me)
-    sources, receivers = own_onsets(onsets_source, me), own_onsets(onsets_receiver, me)
-    u_own = masked(u_factors, tile_ranks)
+    rank = tile_ranks[:, 0, :, None, None]
+    mask = (lax.broadcasted_iota(jnp.int32, (1, 1, RMAX, 2 * FOCAL), 2) < rank).astype(BF)
+    index, mask = lax.optimization_barrier((index, mask))
 
     plus = ()
     for _ in range(ITERS):
-        z = project(index, v_factors, plus, direct_field)
-        image = exchange(expand(True, route(z), u_own))
+        z = project(True, index, direct_field, v_factors, plus)
+        image = expand(True, route(z), u_factors, mask)
+        if not plus:
+            image, me = lax.optimization_barrier((image, me))
+            tables = own_tables(me)
+            sources, receivers = own_onsets(onsets_source, me), own_onsets(onsets_receiver, me)
+        image = exchange(image)
         minus = exchange(window(image, sources, tables))
-        w = project(index, u_own, minus)
+        w = project(False, index, mask, u_factors, minus)
         image = exchange(expand(False, route(w), v_factors))
         plus = exchange(window(image, receivers, tables))
     return (finish(index, plus, direct_field), finish(index, minus))

time: 231 us -> 229 us (level)
  blocking collectives: 100 us -> 140 us
  waiting for transfers between devices: 52.4 us -> 30.3 us
  starting transfers between devices: 48.8 us -> 36.5 us
  local copies, waits for them, and re-layouts: 10.6 us -> 4.14 us
    all_to_all x3 -> x4, blocking collectives: 100 us -> 140 us  [route(): lax.all_to_all(z.reshape(TILES, OWN * RMAX, 2 * FOCAL), 'tile', 0, 0, til...]
    all_to_all x1 -> x0, waiting for transfers between devices: 21.9 us -> none  [route(): lax.all_to_all(z.reshape(TILES, OWN * RMAX, 2 * FOCAL), 'tile', 0, 0, til...]
    all_to_all x1 -> x0, starting transfers between devices: 12.1 us -> none  [route(): lax.all_to_all(z.reshape(TILES, OWN * RMAX, 2 * FOCAL), 'tile', 0, 0, til...]
    unnamed x24 -> x18, local copies, waits for them, and re-layouts: 9.61 us -> 3.26 us
  transfers between devices with their start and end apart: 25 -> 24, of which waited for: 25 -> 23; matrix products, arithmetic and copies ran while one was open for 1% -> 0% of each run, Pallas kernels for 1% -> 0%
where the time goes in v2:
time: 229 us; the launch traced here: 228 us
  blocking collectives  140 us (61%)
  starting transfers between devices  36.5 us (16%)
  waiting for transfers between devices  30.3 us (13%)
  Pallas kernels  15.9 us (7%)
  local copies, waits for them, and re-layouts  4.14 us (2%)
    all_to_all x4, blocking collectives, route(): lax.all_to_all(z.reshape(TILES, OWN * RMAX, 2 * FOCAL), 'tile', 0, 0, til...  140 us
    ppermute x24, starting transfers between devices, exchange(): lax.ppermute(parts[r], 'freq', [(i, (i + r) % GROUPS) for i in range(GROU...  36.5 us
    ppermute x24, waiting for transfers between devices, exchange(): lax.ppermute(parts[r], 'freq', [(i, (i + r) % GROUPS) for i in range(GROU...  30.3 us
    pallas_call x4, Pallas kernels, window(): pl.pallas_call(window_kernel, in_specs=vmem(GROUPS + 3), out_specs=vmem(G...  6.2 us
    pallas_call x4, Pallas kernels, project(): pl.pallas_call(functools.partial(project_kernel, forward, len(field) > 0)...  5.03 us
  transfers between devices with their start and end apart: 24, of which 23 were waited for; matrix products, arithmetic and copies ran while one was open for 0% of the time, Pallas kernels for 0%

profile of v2, /device:TPU:8, one launch (start us, length us, event | category | flops | bytes accessed | tf_op | source)
XLA Modules:
  0.0 228.4 jit_solution(13758334270442129396)
XLA Ops:
  0.6 1.0 fusion.outs_0_.refs_0_
  1.7 2.2 copy-done.1
  3.9 1.0 copy-done.5
  4.9 1.2 project.4
  6.2 39.2 %all_to_all.20 = bf16[64,64,128]{2,1,0:T(8,128)(2,1)S(1)} all-to-all(bf16[64,64,128]{2,1,0:T(8,128)(2,1)S(1)} %bitcast.17), channel_id=1, replica_groups=mesh['freq'=4,'tile'=64] {'tile'}, dimensions={0} | all-to-all | bytes 2097152 | tf_op jit(solution)/shard_map/all_to_all | solution.py:246
  46.2 1.6 collective-permute-start
  47.7 2.7 %collective-permute-start.1 = (bf16[4,2,16,256]{3,2,1,0:T(8,128)(2,1)S(1)}, bf16[4,2,16,256]{3,2,1,0:T(8,128)(2,1)S(1)}, u32[]{:S(2)}, u32[]{:S(2)}) collective-permute-start(bf16[4,2,16,256]{3,2,1,0:T(8,128)(2,1)S(1)} %get-tuple-element.49), channel_id=1, source_target_pairs={{0,128},{64,192},{128,0},{192,64},{1,129},{65,193},{129,1},{193,65... | collective-permute-start | bytes 196616 | tf_op jit(solution)/shard_map/ppermute | solution.py:235
  50.5 1.4 collective-permute-start.2
  52.1 2.3 %collective-permute-done.1.s2 = bf16[4,2,16,256]{3,2,1,0:T(8,128)(2,1)S(1)} collective-permute-done((bf16[4,2,16,256]{3,2,1,0:T(8,128)(2,1)S(1)}, bf16[4,2,16,256]{3,2,1,0:T(8,128)(2,1)S(1)}, u32[]{:S(2)}, u32[]{:S(2)}) %collective-permute-start.1) | collective-permute-done | bytes 65568 | tf_op jit(solution)/shard_map/ppermute | solution.py:235
  55.3 1.5 window.4
  56.9 1.4 collective-permute-start.3
  58.2 2.8 %collective-permute-start.4 = (bf16[4,2,16,256]{3,2,1,0:T(8,128)(2,1)S(1)}, bf16[4,2,16,256]{3,2,1,0:T(8,128)(2,1)S(1)}, u32[]{:S(2)}, u32[]{:S(2)}) collective-permute-start(bf16[4,2,16,256]{3,2,1,0:T(8,128)(2,1)S(1)} %get-tuple-element.54), channel_id=1, source_target_pairs={{0,128},{64,192},{128,0},{192,64},{1,129},{65,193},{129,1},{193,65... | collective-permute-start | bytes 196616 | tf_op jit(solution)/shard_map/ppermute | solution.py:235
  61.8 0.9 collective-permute-done.3.refs_3_
  62.7 1.7 collective-permute-done.4.refs_4_
  64.4 0.9 collective-permute-done.5.refs_5_
  65.3 1.3 project.5
  66.6 34.0 %all_to_all.21 = bf16[64,64,128]{2,1,0:T(8,128)(2,1)S(1)} all-to-all(bf16[64,64,128]{2,1,0:T(8,128)(2,1)S(1)} %bitcast.14), channel_id=1, replica_groups=mesh['freq'=4,'tile'=64] {'tile'}, dimensions={0} | all-to-all | bytes 2097152 | tf_op jit(solution)/shard_map/all_to_all | solution.py:246
  101.4 2.9 %collective-permute-start.7 = (bf16[4,2,16,256]{3,2,1,0:T(8,128)(2,1)S(1)}, bf16[4,2,16,256]{3,2,1,0:T(8,128)(2,1)S(1)}, u32[]{:S(2)}, u32[]{:S(2)}) collective-permute-start(bf16[4,2,16,256]{3,2,1,0:T(8,128)(2,1)S(1)} %get-tuple-element.58), channel_id=1, source_target_pairs={{0,128},{64,192},{128,0},{192,64},{1,129},{65,193},{129,1},{193,65... | collective-permute-start | bytes 196616 | tf_op jit(solution)/shard_map/ppermute | solution.py:235
  104.3 1.2 collective-permute-start.8
  106.3 1.3 collective-permute-done.6.s1
  108.4 1.3 collective-permute-done.8.s3
  109.7 1.6 window.5
  111.2 1.1 collective-permute-start.9
  112.4 3.2 %collective-permute-start.10 = (bf16[4,2,16,256]{3,2,1,0:T(8,128)(2,1)S(1)}, bf16[4,2,16,256]{3,2,1,0:T(8,128)(2,1)S(1)}, u32[]{:S(2)}, u32[]{:S(2)}) collective-permute-start(bf16[4,2,16,256]{3,2,1,0:T(8,128)(2,1)S(1)} %get-tuple-element.62), channel_id=1, source_target_pairs={{0,128},{64,192},{128,0},{192,64},{1,129},{65,193},{129,1},{193,65... | collective-permute-start | bytes 196616 | tf_op jit(solution)/shard_map/ppermute | solution.py:235
  115.6 1.2 collective-permute-done.9.refs_3_
  116.8 2.3 %collective-permute-done.10.refs_4_ = bf16[4,2,16,256]{3,2,1,0:T(8,128)(2,1)S(1)} collective-permute-done((bf16[4,2,16,256]{3,2,1,0:T(8,128)(2,1)S(1)}, bf16[4,2,16,256]{3,2,1,0:T(8,128)(2,1)S(1)}, u32[]{:S(2)}, u32[]{:S(2)}) %collective-permute-start.10) | collective-permute-done | bytes 65568 | tf_op jit(solution)/shard_map/ppermute | solution.py:235
  119.9 1.3 project.6
  121.1 33.2 %all_to_all.22 = bf16[64,64,128]{2,1,0:T(8,128)(2,1)S(1)} all-to-all(bf16[64,64,128]{2,1,0:T(8,128)(2,1)S(1)} %bitcast.15), channel_id=1, replica_groups=mesh['freq'=4,'tile'=64] {'tile'}, dimensions={0} | all-to-all | bytes 2097152 | tf_op jit(solution)/shard_map/all_to_all | solution.py:246
  155.2 2.9 %collective-permute-start.13 = (bf16[4,2,16,256]{3,2,1,0:T(8,128)(2,1)S(1)}, bf16[4,2,16,256]{3,2,1,0:T(8,128)(2,1)S(1)}, u32[]{:S(2)}, u32[]{:S(2)}) collective-permute-start(bf16[4,2,16,256]{3,2,1,0:T(8,128)(2,1)S(1)} %get-tuple-element.66), channel_id=1, source_target_pairs={{0,128},{64,192},{128,0},{192,64},{1,129},{65,193},{129,1},{193,65... | collective-permute-start | bytes 196616 | tf_op jit(solution)/shard_map/ppermute | solution.py:235
  158.1 1.3 collective-permute-start.14
  159.4 2.0 collective-permute-done.12.s1
  162.2 1.3 collective-permute-done.14.s3
  163.5 1.5 window.6
  165.1 1.2 collective-permute-start.15
  166.2 3.2 %collective-permute-start.16 = (bf16[4,2,16,256]{3,2,1,0:T(8,128)(2,1)S(1)}, bf16[4,2,16,256]{3,2,1,0:T(8,128)(2,1)S(1)}, u32[]{:S(2)}, u32[]{:S(2)}) collective-permute-start(bf16[4,2,16,256]{3,2,1,0:T(8,128)(2,1)S(1)} %get-tuple-element.70), channel_id=1, source_target_pairs={{0,128},{64,192},{128,0},{192,64},{1,129},{65,193},{129,1},{193,65... | collective-permute-start | bytes 196616 | tf_op jit(solution)/shard_map/ppermute | solution.py:235
  169.4 1.2 collective-permute-done.15.refs_3_.refs_2_
  170.6 2.3 %collective-permute-done.16.refs_4_.refs_3_ = bf16[4,2,16,256]{3,2,1,0:T(8,128)(2,1)S(1)} collective-permute-done((bf16[4,2,16,256]{3,2,1,0:T(8,128)(2,1)S(1)}, bf16[4,2,16,256]{3,2,1,0:T(8,128)(2,1)S(1)}, u32[]{:S(2)}, u32[]{:S(2)}) %collective-permute-start.16) | collective-permute-done | bytes 65568 | tf_op jit(solution)/shard_map/ppermute | solution.py:235
  173.7 1.3 project.7
  175.0 33.2 %all_to_all.23 = bf16[64,64,128]{2,1,0:T(8,128)(2,1)S(1)} all-to-all(bf16[64,64,128]{2,1,0:T(8,128)(2,1)S(1)} %bitcast.16), channel_id=1, replica_groups=mesh['freq'=4,'tile'=64] {'tile'}, dimensions={0} | all-to-all | bytes 2097152 | tf_op jit(solution)/shard_map/all_to_all | solution.py:246
  209.1 3.0 %collective-permute-start.19 = (bf16[4,2,16,256]{3,2,1,0:T(8,128)(2,1)S(1)}, bf16[4,2,16,256]{3,2,1,0:T(8,128)(2,1)S(1)}, u32[]{:S(2)}, u32[]{:S(2)}) collective-permute-start(bf16[4,2,16,256]{3,2,1,0:T(8,128)(2,1)S(1)} %get-tuple-element.74), channel_id=1, source_target_pairs={{0,128},{64,192},{128,0},{192,64},{1,129},{65,193},{129,1},{193,65... | collective-permute-start | bytes 196616 | tf_op jit(solution)/shard_map/ppermute | solution.py:235
  212.1 1.1 collective-permute-start.20
  213.2 1.9 collective-permute-done.18.s1
  215.1 1.1 collective-permute-done.19.s2
  216.2 1.2 collective-permute-done.20.s3
  217.3 1.6 window.7
  218.9 1.1 collective-permute-start.21
  220.0 3.2 %collective-permute-start.22 = (bf16[4,2,16,256]{3,2,1,0:T(8,128)(2,1)S(1)}, bf16[4,2,16,256]{3,2,1,0:T(8,128)(2,1)S(1)}, u32[]{:S(2)}, u32[]{:S(2)}) collective-permute-start(bf16[4,2,16,256]{3,2,1,0:T(8,128)(2,1)S(1)} %get-tuple-element.78), channel_id=1, source_target_pairs={{0,128},{64,192},{128,0},{192,64},{1,129},{65,193},{129,1},{193,65... | collective-permute-start | bytes 196616 | tf_op jit(solution)/shard_map/ppermute | solution.py:235
  224.5 2.3 %collective-permute-done.22.refs_4_ = bf16[4,2,16,256]{3,2,1,0:T(8,128)(2,1)S(1)} collective-permute-done((bf16[4,2,16,256]{3,2,1,0:T(8,128)(2,1)S(1)}, bf16[4,2,16,256]{3,2,1,0:T(8,128)(2,1)S(1)}, u32[]{:S(2)}, u32[]{:S(2)}) %collective-permute-start.22) | collective-permute-done | bytes 65568 | tf_op jit(solution)/shard_map/ppermute | solution.py:235
  (40 shorter events, 11.9 us)
Async XLA Ops:
  0.6 51.4 %copy-start = (s32[64,256]{1,0:T(8,128)S(1)}, s32[64,256]{1,0:T(8,128)}, u32[]{:S(2)}) copy-start(s32[64,256]{1,0:T(8,128)} %param.12) | copy-start | bytes 196612
  1.7 2.2 copy-start.1
  3.9 1.0 copy-start.5
  4.9 40.5 %copy-start.3 = (bf16[4,1,64,2,16,256]{5,4,3,2,1,0:T(8,128)(2,1)S(1)}, bf16[4,1,64,2,16,256]{5,4,3,2,1,0:T(8,128)(2,1)}, u32[]{:S(2)}) copy-start(bf16[4,1,64,2,16,256]{5,4,3,2,1,0:T(8,128)(2,1)} %refs_1_.8) | copy-start | bytes 12582916
  6.2 45.7 %copy-start.7 = (bf16[2,448,256]{2,1,0:T(8,128)(2,1)S(1)}, bf16[2,448,256]{2,1,0:T(8,128)(2,1)}, u32[]{:S(2)}) copy-start(bf16[2,448,256]{2,1,0:T(8,128)(2,1)} %constant.21.clone) | copy-start | bytes 1376260
  6.2 45.7 %copy-start.8 = (bf16[2,256,448]{2,1,0:T(8,128)(2,1)S(1)}, bf16[2,256,448]{2,1,0:T(8,128)(2,1)}, u32[]{:S(2)}) copy-start(bf16[2,256,448]{2,1,0:T(8,128)(2,1)} %constant.20.clone) | copy-start | bytes 1376260
  46.2 5.9 %collective-permute-start = (bf16[4,2,16,256]{3,2,1,0:T(8,128)(2,1)S(1)}, bf16[4,2,16,256]{3,2,1,0:T(8,128)(2,1)S(1)}, u32[]{:S(2)}, u32[]{:S(2)}) collective-permute-start(bf16[4,2,16,256]{3,2,1,0:T(8,128)(2,1)S(1)} %get-tuple-element.48), channel_id=1, source_target_pairs={{0,64},{64,128},{128,192},{192,0},{1,65},{65,129},{129,193},{193,1... | collective-permute-start | bytes 196616 | tf_op jit(solution)/shard_map/ppermute | solution.py:235
  47.7 6.7 %collective-permute-start.1 = (bf16[4,2,16,256]{3,2,1,0:T(8,128)(2,1)S(1)}, bf16[4,2,16,256]{3,2,1,0:T(8,128)(2,1)S(1)}, u32[]{:S(2)}, u32[]{:S(2)}) collective-permute-start(bf16[4,2,16,256]{3,2,1,0:T(8,128)(2,1)S(1)} %get-tuple-element.49), channel_id=1, source_target_pairs={{0,128},{64,192},{128,0},{192,64},{1,129},{65,193},{129,1},{193,65... | collective-permute-start | bytes 196616 | tf_op jit(solution)/shard_map/ppermute | solution.py:235
  50.5 4.8 %collective-permute-start.2 = (bf16[4,2,16,256]{3,2,1,0:T(8,128)(2,1)S(1)}, bf16[4,2,16,256]{3,2,1,0:T(8,128)(2,1)S(1)}, u32[]{:S(2)}, u32[]{:S(2)}) collective-permute-start(bf16[4,2,16,256]{3,2,1,0:T(8,128)(2,1)S(1)} %get-tuple-element.50), channel_id=1, source_target_pairs={{0,192},{64,0},{128,64},{192,128},{1,193},{65,1},{129,65},{193,129... | collective-permute-start | bytes 196616 | tf_op jit(solution)/shard_map/ppermute | solution.py:235
  51.9 13.4 %copy-start.4 = (bf16[4,1,64,2,16,256]{5,4,3,2,1,0:T(8,128)(2,1)S(1)}, bf16[4,1,64,2,16,256]{5,4,3,2,1,0:T(8,128)(2,1)}, u32[]{:S(2)}) copy-start(bf16[4,1,64,2,16,256]{5,4,3,2,1,0:T(8,128)(2,1)} %refs_1_.8) | copy-start | bytes 12582916
  56.9 5.9 %collective-permute-start.3 = (bf16[4,2,16,256]{3,2,1,0:T(8,128)(2,1)S(1)}, bf16[4,2,16,256]{3,2,1,0:T(8,128)(2,1)S(1)}, u32[]{:S(2)}, u32[]{:S(2)}) collective-permute-start(bf16[4,2,16,256]{3,2,1,0:T(8,128)(2,1)S(1)} %get-tuple-element.53), channel_id=1, source_target_pairs={{0,64},{64,128},{128,192},{192,0},{1,65},{65,129},{129,193},{193,1... | collective-permute-start | bytes 196616 | tf_op jit(solution)/shard_map/ppermute | solution.py:235
  58.2 6.2 %collective-permute-start.4 = (bf16[4,2,16,256]{3,2,1,0:T(8,128)(2,1)S(1)}, bf16[4,2,16,256]{3,2,1,0:T(8,128)(2,1)S(1)}, u32[]{:S(2)}, u32[]{:S(2)}) collective-permute-start(bf16[4,2,16,256]{3,2,1,0:T(8,128)(2,1)S(1)} %get-tuple-element.54), channel_id=1, source_target_pairs={{0,128},{64,192},{128,0},{192,64},{1,129},{65,193},{129,1},{193,65... | collective-permute-start | bytes 196616 | tf_op jit(solution)/shard_map/ppermute | solution.py:235
  61.0 4.3 %collective-permute-start.5 = (bf16[4,2,16,256]{3,2,1,0:T(8,128)(2,1)S(1)}, bf16[4,2,16,256]{3,2,1,0:T(8,128)(2,1)S(1)}, u32[]{:S(2)}, u32[]{:S(2)}) collective-permute-start(bf16[4,2,16,256]{3,2,1,0:T(8,128)(2,1)S(1)} %get-tuple-element.55), channel_id=1, source_target_pairs={{0,192},{64,0},{128,64},{192,128},{1,193},{65,1},{129,65},{193,129... | collective-permute-start | bytes 196616 | tf_op jit(solution)/shard_map/ppermute | solution.py:235
  65.3 35.2 %copy-start.2 = (bf16[4,64,1,2,16,256]{5,4,3,2,1,0:T(8,128)(2,1)S(1)}, bf16[4,64,1,2,16,256]{5,4,3,2,1,0:T(8,128)(2,1)}, u32[]{:S(2)}) copy-start(bf16[4,64,1,2,16,256]{5,4,3,2,1,0:T(8,128)(2,1)} %f_ref.7) | copy-start | bytes 12582916
  100.6 19.3 %copy-start.6 = (f32[4,2,64,256]{3,2,1,0:T(8,128)S(1)}, f32[4,2,64,256]{3,2,1,0:T(8,128)}, u32[]{:S(2)}) copy-start(f32[4,2,64,256]{3,2,1,0:T(8,128)} %refs_1_.9) | copy-start | bytes 1572868
  101.3 6.2 %collective-permute-start.6 = (bf16[4,2,16,256]{3,2,1,0:T(8,128)(2,1)S(1)}, bf16[4,2,16,256]{3,2,1,0:T(8,128)(2,1)S(1)}, u32[]{:S(2)}, u32[]{:S(2)}) collective-permute-start(bf16[4,2,16,256]{3,2,1,0:T(8,128)(2,1)S(1)} %get-tuple-element.57), channel_id=1, source_target_pairs={{0,64},{64,128},{128,192},{192,0},{1,65},{65,129},{129,193},{193,1... | collective-permute-start | bytes 196616 | tf_op jit(solution)/shard_map/ppermute | solution.py:235
  101.4 7.0 %collective-permute-start.7 = (bf16[4,2,16,256]{3,2,1,0:T(8,128)(2,1)S(1)}, bf16[4,2,16,256]{3,2,1,0:T(8,128)(2,1)S(1)}, u32[]{:S(2)}, u32[]{:S(2)}) collective-permute-start(bf16[4,2,16,256]{3,2,1,0:T(8,128)(2,1)S(1)} %get-tuple-element.58), channel_id=1, source_target_pairs={{0,128},{64,192},{128,0},{192,64},{1,129},{65,193},{129,1},{193,65... | collective-permute-start | bytes 196616 | tf_op jit(solution)/shard_map/ppermute | solution.py:235
  104.3 5.4 %collective-permute-start.8 = (bf16[4,2,16,256]{3,2,1,0:T(8,128)(2,1)S(1)}, bf16[4,2,16,256]{3,2,1,0:T(8,128)(2,1)S(1)}, u32[]{:S(2)}, u32[]{:S(2)}) collective-permute-start(bf16[4,2,16,256]{3,2,1,0:T(8,128)(2,1)S(1)} %get-tuple-element.59), channel_id=1, source_target_pairs={{0,192},{64,0},{128,64},{192,128},{1,193},{65,1},{129,65},{193,129... | collective-permute-start | bytes 196616 | tf_op jit(solution)/shard_map/ppermute | solution.py:235
  111.2 5.6 %collective-permute-start.9 = (bf16[4,2,16,256]{3,2,1,0:T(8,128)(2,1)S(1)}, bf16[4,2,16,256]{3,2,1,0:T(8,128)(2,1)S(1)}, u32[]{:S(2)}, u32[]{:S(2)}) collective-permute-start(bf16[4,2,16,256]{3,2,1,0:T(8,128)(2,1)S(1)} %get-tuple-element.61), channel_id=1, source_target_pairs={{0,64},{64,128},{128,192},{192,0},{1,65},{65,129},{129,193},{193,1... | collective-permute-start | bytes 196616 | tf_op jit(solution)/shard_map/ppermute | solution.py:235
  112.4 6.7 %collective-permute-start.10 = (bf16[4,2,16,256]{3,2,1,0:T(8,128)(2,1)S(1)}, bf16[4,2,16,256]{3,2,1,0:T(8,128)(2,1)S(1)}, u32[]{:S(2)}, u32[]{:S(2)}) collective-permute-start(bf16[4,2,16,256]{3,2,1,0:T(8,128)(2,1)S(1)} %get-tuple-element.62), channel_id=1, source_target_pairs={{0,128},{64,192},{128,0},{192,64},{1,129},{65,193},{129,1},{193,65... | collective-permute-start | bytes 196616 | tf_op jit(solution)/shard_map/ppermute | solution.py:235
  115.6 4.3 %collective-permute-start.11 = (bf16[4,2,16,256]{3,2,1,0:T(8,128)(2,1)S(1)}, bf16[4,2,16,256]{3,2,1,0:T(8,128)(2,1)S(1)}, u32[]{:S(2)}, u32[]{:S(2)}) collective-permute-start(bf16[4,2,16,256]{3,2,1,0:T(8,128)(2,1)S(1)} %get-tuple-element.63), channel_id=1, source_target_pairs={{0,192},{64,0},{128,64},{192,128},{1,193},{65,1},{129,65},{193,129... | collective-permute-start | bytes 196616 | tf_op jit(solution)/shard_map/ppermute | solution.py:235
  155.2 6.2 %collective-permute-start.12 = (bf16[4,2,16,256]{3,2,1,0:T(8,128)(2,1)S(1)}, bf16[4,2,16,256]{3,2,1,0:T(8,128)(2,1)S(1)}, u32[]{:S(2)}, u32[]{:S(2)}) collective-permute-start(bf16[4,2,16,256]{3,2,1,0:T(8,128)(2,1)S(1)} %get-tuple-element.65), channel_id=1, source_target_pairs={{0,64},{64,128},{128,192},{192,0},{1,65},{65,129},{129,193},{193,1... | collective-permute-start | bytes 196616 | tf_op jit(solution)/shard_map/ppermute | solution.py:235
  155.2 7.0 %collective-permute-start.13 = (bf16[4,2,16,256]{3,2,1,0:T(8,128)(2,1)S(1)}, bf16[4,2,16,256]{3,2,1,0:T(8,128)(2,1)S(1)}, u32[]{:S(2)}, u32[]{:S(2)}) collective-permute-start(bf16[4,2,16,256]{3,2,1,0:T(8,128)(2,1)S(1)} %get-tuple-element.66), channel_id=1, source_target_pairs={{0,128},{64,192},{128,0},{192,64},{1,129},{65,193},{129,1},{193,65... | collective-permute-start | bytes 196616 | tf_op jit(solution)/shard_map/ppermute | solution.py:235
  158.1 5.4 %collective-permute-start.14 = (bf16[4,2,16,256]{3,2,1,0:T(8,128)(2,1)S(1)}, bf16[4,2,16,256]{3,2,1,0:T(8,128)(2,1)S(1)}, u32[]{:S(2)}, u32[]{:S(2)}) collective-permute-start(bf16[4,2,16,256]{3,2,1,0:T(8,128)(2,1)S(1)} %get-tuple-element.67), channel_id=1, source_target_pairs={{0,192},{64,0},{128,64},{192,128},{1,193},{65,1},{129,65},{193,129... | collective-permute-start | bytes 196616 | tf_op jit(solution)/shard_map/ppermute | solution.py:235
  165.1 5.6 %collective-permute-start.15 = (bf16[4,2,16,256]{3,2,1,0:T(8,128)(2,1)S(1)}, bf16[4,2,16,256]{3,2,1,0:T(8,128)(2,1)S(1)}, u32[]{:S(2)}, u32[]{:S(2)}) collective-permute-start(bf16[4,2,16,256]{3,2,1,0:T(8,128)(2,1)S(1)} %get-tuple-element.69), channel_id=1, source_target_pairs={{0,64},{64,128},{128,192},{192,0},{1,65},{65,129},{129,193},{193,1... | collective-permute-start | bytes 196616 | tf_op jit(solution)/shard_map/ppermute | solution.py:235
  166.2 6.7 %collective-permute-start.16 = (bf16[4,2,16,256]{3,2,1,0:T(8,128)(2,1)S(1)}, bf16[4,2,16,256]{3,2,1,0:T(8,128)(2,1)S(1)}, u32[]{:S(2)}, u32[]{:S(2)}) collective-permute-start(bf16[4,2,16,256]{3,2,1,0:T(8,128)(2,1)S(1)} %get-tuple-element.70), channel_id=1, source_target_pairs={{0,128},{64,192},{128,0},{192,64},{1,129},{65,193},{129,1},{193,65... | collective-permute-start | bytes 196616 | tf_op jit(solution)/shard_map/ppermute | solution.py:235
  169.4 4.3 %collective-permute-start.17 = (bf16[4,2,16,256]{3,2,1,0:T(8,128)(2,1)S(1)}, bf16[4,2,16,256]{3,2,1,0:T(8,128)(2,1)S(1)}, u32[]{:S(2)}, u32[]{:S(2)}) collective-permute-start(bf16[4,2,16,256]{3,2,1,0:T(8,128)(2,1)S(1)} %get-tuple-element.71), channel_id=1, source_target_pairs={{0,192},{64,0},{128,64},{192,128},{1,193},{65,1},{129,65},{193,129... | collective-permute-start | bytes 196616 | tf_op jit(solution)/shard_map/ppermute | solution.py:235
  209.0 6.1 %collective-permute-start.18 = (bf16[4,2,16,256]{3,2,1,0:T(8,128)(2,1)S(1)}, bf16[4,2,16,256]{3,2,1,0:T(8,128)(2,1)S(1)}, u32[]{:S(2)}, u32[]{:S(2)}) collective-permute-start(bf16[4,2,16,256]{3,2,1,0:T(8,128)(2,1)S(1)} %get-tuple-element.73), channel_id=1, source_target_pairs={{0,64},{64,128},{128,192},{192,0},{1,65},{65,129},{129,193},{193,1... | collective-permute-start | bytes 196616 | tf_op jit(solution)/shard_map/ppermute | solution.py:235
  209.1 7.1 %collective-permute-start.19 = (bf16[4,2,16,256]{3,2,1,0:T(8,128)(2,1)S(1)}, bf16[4,2,16,256]{3,2,1,0:T(8,128)(2,1)S(1)}, u32[]{:S(2)}, u32[]{:S(2)}) collective-permute-start(bf16[4,2,16,256]{3,2,1,0:T(8,128)(2,1)S(1)} %get-tuple-element.74), channel_id=1, source_target_pairs={{0,128},{64,192},{128,0},{192,64},{1,129},{65,193},{129,1},{193,65... | collective-permute-start | bytes 196616 | tf_op jit(solution)/shard_map/ppermute | solution.py:235
  212.1 5.3 %collective-permute-start.20 = (bf16[4,2,16,256]{3,2,1,0:T(8,128)(2,1)S(1)}, bf16[4,2,16,256]{3,2,1,0:T(8,128)(2,1)S(1)}, u32[]{:S(2)}, u32[]{:S(2)}) collective-permute-start(bf16[4,2,16,256]{3,2,1,0:T(8,128)(2,1)S(1)} %get-tuple-element.75), channel_id=1, source_target_pairs={{0,192},{64,0},{128,64},{192,128},{1,193},{65,1},{129,65},{193,129... | collective-permute-start | bytes 196616 | tf_op jit(solution)/shard_map/ppermute | solution.py:235
  218.9 5.6 %collective-permute-start.21 = (bf16[4,2,16,256]{3,2,1,0:T(8,128)(2,1)S(1)}, bf16[4,2,16,256]{3,2,1,0:T(8,128)(2,1)S(1)}, u32[]{:S(2)}, u32[]{:S(2)}) collective-permute-start(bf16[4,2,16,256]{3,2,1,0:T(8,128)(2,1)S(1)} %get-tuple-element.77), channel_id=1, source_target_pairs={{0,64},{64,128},{128,192},{192,0},{1,65},{65,129},{129,193},{193,1... | collective-permute-start | bytes 196616 | tf_op jit(solution)/shard_map/ppermute | solution.py:235
  220.0 6.7 %collective-permute-start.22 = (bf16[4,2,16,256]{3,2,1,0:T(8,128)(2,1)S(1)}, bf16[4,2,16,256]{3,2,1,0:T(8,128)(2,1)S(1)}, u32[]{:S(2)}, u32[]{:S(2)}) collective-permute-start(bf16[4,2,16,256]{3,2,1,0:T(8,128)(2,1)S(1)} %get-tuple-element.78), channel_id=1, source_target_pairs={{0,128},{64,192},{128,0},{192,64},{1,129},{65,193},{129,1},{193,65... | collective-permute-start | bytes 196616 | tf_op jit(solution)/shard_map/ppermute | solution.py:235
  223.3 4.3 %collective-permute-start.23 = (bf16[4,2,16,256]{3,2,1,0:T(8,128)(2,1)S(1)}, bf16[4,2,16,256]{3,2,1,0:T(8,128)(2,1)S(1)}, u32[]{:S(2)}, u32[]{:S(2)}) collective-permute-start(bf16[4,2,16,256]{3,2,1,0:T(8,128)(2,1)S(1)} %get-tuple-element.79), channel_id=1, source_target_pairs={{0,192},{64,0},{128,64},{192,128},{1,193},{65,1},{129,65},{193,129... | collective-permute-start | bytes 196616 | tf_op jit(solution)/shard_map/ppermute | solution.py:235

commit v3 on v2

--- a/solution.py
+++ b/solution.py
@@ -120,23 +120,18 @@
     half = PW // 2
     rows = OWN * 2 * PW
     count = GROUPS * rows
-    lane = lax.broadcasted_iota(jnp.int32, (1, count), 1) % PW
-    row = lax.broadcasted_iota(jnp.int32, (count, 1), 0) % PW
+    lane = lax.broadcasted_iota(jnp.int32, (1, count), 1) % half
+    row = lax.broadcasted_iota(jnp.int32, (count, 1), 0) % half
     first = lax.broadcasted_iota(jnp.int32, (count, TILE), 0) % PW < half
     moment = lax.broadcasted_iota(jnp.int32, (SAMPLES, TILE), 0)
 
     def one(flags):
         return flags.astype(F32).astype(BF)
 
-    inverse, forward = [], []
-    for part in range(2):
-        points = [(p, (p + half) % PW) for p in range(part * half, (part + 1) * half)]
-        inverse.append(
-            jnp.concatenate([t_ref[0] * one(lane == p) + t_ref[1] * one(lane == o) for p, o in points], axis=0)
-        )
-        forward.append(
-            jnp.concatenate([f_ref[0] * one(row == p) + f_ref[1] * one(row == o) for p, o in points], axis=1)
-        )
+    lanes = [one(lane == p) for p in range(half)]
+    rows_of = [one(row == p) for p in range(half)]
+    inverse = [jnp.concatenate([t_ref[part] * pick for pick in lanes], axis=0) for part in range(2)]
+    forward = [jnp.concatenate([f_ref[part] * pick for pick in rows_of], axis=1) for part in range(2)]
     for g in range(SETS):
         whole = jnp.concatenate(
             [ref[:, g].reshape(rows, TILE) for ref in (s0, s1, s2, s3)], axis=0
@@ -217,7 +212,13 @@
     spread = np.repeat(paired.reshape(GROUPS, OWN, 2, 1, SAMPLES), PW, axis=3)
     order = [3, 2, 1, 0, 3, 2, 1]
     rows = spread[order].reshape(len(order) * OWN * 2 * PW, SAMPLES)
-    return split_bf16(np.ascontiguousarray(rows.T)), split_bf16(2.0 / SAMPLES * rows)
+    early = (np.arange(rows.shape[0]) % PW < PW // 2)[:, None]
+
+    def halves(table):
+        high, low = split_bf16(table)
+        return np.stack([np.where(early, high, low), np.where(early, low, high)])
+
+    return np.ascontiguousarray(halves(rows).transpose(0, 2, 1)), halves(2.0 / SAMPLES * rows)
 
 
 def own_tables(me):

time: 229 us -> 228 us (level)
  no operation moved by 1% of the time
where the time goes in v3:
time: 228 us
  blocking collectives  140 us (61%)
  starting transfers between devices  36.5 us (16%)
  waiting for transfers between devices  30.3 us (13%)
  Pallas kernels  15.6 us (7%)
  local copies, waits for them, and re-layouts  4.14 us (2%)
    all_to_all x4, blocking collectives, route(): lax.all_to_all(z.reshape(TILES, OWN * RMAX, 2 * FOCAL), 'tile', 0, 0, til...  140 us
    ppermute x24, starting transfers between devices, exchange(): lax.ppermute(parts[r], 'freq', [(i, (i + r) % GROUPS) for i in range(GROU...  36.5 us
    ppermute x24, waiting for transfers between devices, exchange(): lax.ppermute(parts[r], 'freq', [(i, (i + r) % GROUPS) for i in range(GROU...  30.3 us
    pallas_call x4, Pallas kernels, window(): pl.pallas_call(window_kernel, in_specs=vmem(GROUPS + 3), out_specs=vmem(G...  5.85 us
    pallas_call x4, Pallas kernels, project(): pl.pallas_call(functools.partial(project_kernel, forward, len(field) > 0)...  5.03 us
  transfers between devices with their start and end apart: 24, of which 23 were waited for; matrix products, arithmetic and copies ran while one was open for 0% of the time, Pallas kernels for 0%

profile of v3, /device:TPU:8, one launch (start us, length us, event | category | flops | bytes accessed | tf_op | source)
XLA Modules:
  0.0 228.1 jit_solution(4375745055657161986)
XLA Ops:
  0.6 1.0 fusion.outs_0_.refs_0_
  1.7 2.2 copy-done.1
  3.9 1.0 copy-done.5
  4.9 1.2 project.4
  6.2 39.2 %all_to_all.20 = bf16[64,64,128]{2,1,0:T(8,128)(2,1)S(1)} all-to-all(bf16[64,64,128]{2,1,0:T(8,128)(2,1)S(1)} %bitcast.17), channel_id=1, replica_groups=mesh['freq'=4,'tile'=64] {'tile'}, dimensions={0} | all-to-all | bytes 2097152 | tf_op jit(solution)/shard_map/all_to_all | solution.py:247
  46.2 1.6 collective-permute-start
  47.7 2.7 %collective-permute-start.1 = (bf16[4,2,16,256]{3,2,1,0:T(8,128)(2,1)S(1)}, bf16[4,2,16,256]{3,2,1,0:T(8,128)(2,1)S(1)}, u32[]{:S(2)}, u32[]{:S(2)}) collective-permute-start(bf16[4,2,16,256]{3,2,1,0:T(8,128)(2,1)S(1)} %get-tuple-element.49), channel_id=1, source_target_pairs={{0,128},{64,192},{128,0},{192,64},{1,129},{65,193},{129,1},{193,65... | collective-permute-start | bytes 196616 | tf_op jit(solution)/shard_map/ppermute | solution.py:236
  50.5 1.4 collective-permute-start.2
  52.1 2.3 %collective-permute-done.1.s2 = bf16[4,2,16,256]{3,2,1,0:T(8,128)(2,1)S(1)} collective-permute-done((bf16[4,2,16,256]{3,2,1,0:T(8,128)(2,1)S(1)}, bf16[4,2,16,256]{3,2,1,0:T(8,128)(2,1)S(1)}, u32[]{:S(2)}, u32[]{:S(2)}) %collective-permute-start.1) | collective-permute-done | bytes 65568 | tf_op jit(solution)/shard_map/ppermute | solution.py:236
  54.4 0.9 collective-permute-done.2.s3
  55.3 1.5 window.4
  56.8 1.4 collective-permute-start.3
  58.1 2.8 %collective-permute-start.4 = (bf16[4,2,16,256]{3,2,1,0:T(8,128)(2,1)S(1)}, bf16[4,2,16,256]{3,2,1,0:T(8,128)(2,1)S(1)}, u32[]{:S(2)}, u32[]{:S(2)}) collective-permute-start(bf16[4,2,16,256]{3,2,1,0:T(8,128)(2,1)S(1)} %get-tuple-element.54), channel_id=1, source_target_pairs={{0,128},{64,192},{128,0},{192,64},{1,129},{65,193},{129,1},{193,65... | collective-permute-start | bytes 196616 | tf_op jit(solution)/shard_map/ppermute | solution.py:236
  61.8 0.9 collective-permute-done.3.refs_3_
  62.6 1.7 collective-permute-done.4.refs_4_
  64.3 0.9 collective-permute-done.5.refs_5_
  65.2 1.3 project.5
  66.5 34.0 %all_to_all.21 = bf16[64,64,128]{2,1,0:T(8,128)(2,1)S(1)} all-to-all(bf16[64,64,128]{2,1,0:T(8,128)(2,1)S(1)} %bitcast.14), channel_id=1, replica_groups=mesh['freq'=4,'tile'=64] {'tile'}, dimensions={0} | all-to-all | bytes 2097152 | tf_op jit(solution)/shard_map/all_to_all | solution.py:247
  101.3 2.9 %collective-permute-start.7 = (bf16[4,2,16,256]{3,2,1,0:T(8,128)(2,1)S(1)}, bf16[4,2,16,256]{3,2,1,0:T(8,128)(2,1)S(1)}, u32[]{:S(2)}, u32[]{:S(2)}) collective-permute-start(bf16[4,2,16,256]{3,2,1,0:T(8,128)(2,1)S(1)} %get-tuple-element.58), channel_id=1, source_target_pairs={{0,128},{64,192},{128,0},{192,64},{1,129},{65,193},{129,1},{193,65... | collective-permute-start | bytes 196616 | tf_op jit(solution)/shard_map/ppermute | solution.py:236
  104.2 1.2 collective-permute-start.8
  106.2 1.3 collective-permute-done.6.s1
  108.3 1.3 collective-permute-done.8.s3
  109.6 1.5 window.5
  111.1 1.1 collective-permute-start.9
  112.2 3.2 %collective-permute-start.10 = (bf16[4,2,16,256]{3,2,1,0:T(8,128)(2,1)S(1)}, bf16[4,2,16,256]{3,2,1,0:T(8,128)(2,1)S(1)}, u32[]{:S(2)}, u32[]{:S(2)}) collective-permute-start(bf16[4,2,16,256]{3,2,1,0:T(8,128)(2,1)S(1)} %get-tuple-element.62), channel_id=1, source_target_pairs={{0,128},{64,192},{128,0},{192,64},{1,129},{65,193},{129,1},{193,65... | collective-permute-start | bytes 196616 | tf_op jit(solution)/shard_map/ppermute | solution.py:236
  115.4 1.2 collective-permute-done.9.refs_3_
  116.6 2.3 %collective-permute-done.10.refs_4_ = bf16[4,2,16,256]{3,2,1,0:T(8,128)(2,1)S(1)} collective-permute-done((bf16[4,2,16,256]{3,2,1,0:T(8,128)(2,1)S(1)}, bf16[4,2,16,256]{3,2,1,0:T(8,128)(2,1)S(1)}, u32[]{:S(2)}, u32[]{:S(2)}) %collective-permute-start.10) | collective-permute-done | bytes 65568 | tf_op jit(solution)/shard_map/ppermute | solution.py:236
  119.7 1.3 project.6
  121.0 33.2 %all_to_all.22 = bf16[64,64,128]{2,1,0:T(8,128)(2,1)S(1)} all-to-all(bf16[64,64,128]{2,1,0:T(8,128)(2,1)S(1)} %bitcast.15), channel_id=1, replica_groups=mesh['freq'=4,'tile'=64] {'tile'}, dimensions={0} | all-to-all | bytes 2097152 | tf_op jit(solution)/shard_map/all_to_all | solution.py:247
  155.1 2.9 %collective-permute-start.13 = (bf16[4,2,16,256]{3,2,1,0:T(8,128)(2,1)S(1)}, bf16[4,2,16,256]{3,2,1,0:T(8,128)(2,1)S(1)}, u32[]{:S(2)}, u32[]{:S(2)}) collective-permute-start(bf16[4,2,16,256]{3,2,1,0:T(8,128)(2,1)S(1)} %get-tuple-element.66), channel_id=1, source_target_pairs={{0,128},{64,192},{128,0},{192,64},{1,129},{65,193},{129,1},{193,65... | collective-permute-start | bytes 196616 | tf_op jit(solution)/shard_map/ppermute | solution.py:236
  158.0 1.3 collective-permute-start.14
  159.2 2.0 collective-permute-done.12.s1
  162.1 1.3 collective-permute-done.14.s3
  163.4 1.5 window.6
  164.8 1.1 collective-permute-start.15
  166.0 3.2 %collective-permute-start.16 = (bf16[4,2,16,256]{3,2,1,0:T(8,128)(2,1)S(1)}, bf16[4,2,16,256]{3,2,1,0:T(8,128)(2,1)S(1)}, u32[]{:S(2)}, u32[]{:S(2)}) collective-permute-start(bf16[4,2,16,256]{3,2,1,0:T(8,128)(2,1)S(1)} %get-tuple-element.70), channel_id=1, source_target_pairs={{0,128},{64,192},{128,0},{192,64},{1,129},{65,193},{129,1},{193,65... | collective-permute-start | bytes 196616 | tf_op jit(solution)/shard_map/ppermute | solution.py:236
  169.2 1.2 collective-permute-done.15.refs_3_.refs_2_
  170.4 2.3 %collective-permute-done.16.refs_4_.refs_3_ = bf16[4,2,16,256]{3,2,1,0:T(8,128)(2,1)S(1)} collective-permute-done((bf16[4,2,16,256]{3,2,1,0:T(8,128)(2,1)S(1)}, bf16[4,2,16,256]{3,2,1,0:T(8,128)(2,1)S(1)}, u32[]{:S(2)}, u32[]{:S(2)}) %collective-permute-start.16) | collective-permute-done | bytes 65568 | tf_op jit(solution)/shard_map/ppermute | solution.py:236
  173.5 1.3 project.7
  174.7 33.2 %all_to_all.23 = bf16[64,64,128]{2,1,0:T(8,128)(2,1)S(1)} all-to-all(bf16[64,64,128]{2,1,0:T(8,128)(2,1)S(1)} %bitcast.16), channel_id=1, replica_groups=mesh['freq'=4,'tile'=64] {'tile'}, dimensions={0} | all-to-all | bytes 2097152 | tf_op jit(solution)/shard_map/all_to_all | solution.py:247
  208.8 2.9 %collective-permute-start.19 = (bf16[4,2,16,256]{3,2,1,0:T(8,128)(2,1)S(1)}, bf16[4,2,16,256]{3,2,1,0:T(8,128)(2,1)S(1)}, u32[]{:S(2)}, u32[]{:S(2)}) collective-permute-start(bf16[4,2,16,256]{3,2,1,0:T(8,128)(2,1)S(1)} %get-tuple-element.74), channel_id=1, source_target_pairs={{0,128},{64,192},{128,0},{192,64},{1,129},{65,193},{129,1},{193,65... | collective-permute-start | bytes 196616 | tf_op jit(solution)/shard_map/ppermute | solution.py:236
  211.7 1.3 collective-permute-start.20
  212.9 2.0 collective-permute-done.18.s1
  215.8 1.3 collective-permute-done.20.s3
  217.1 1.5 window.7
  218.6 1.1 collective-permute-start.21
  219.7 3.2 %collective-permute-start.22 = (bf16[4,2,16,256]{3,2,1,0:T(8,128)(2,1)S(1)}, bf16[4,2,16,256]{3,2,1,0:T(8,128)(2,1)S(1)}, u32[]{:S(2)}, u32[]{:S(2)}) collective-permute-start(bf16[4,2,16,256]{3,2,1,0:T(8,128)(2,1)S(1)} %get-tuple-element.78), channel_id=1, source_target_pairs={{0,128},{64,192},{128,0},{192,64},{1,129},{65,193},{129,1},{193,65... | collective-permute-start | bytes 196616 | tf_op jit(solution)/shard_map/ppermute | solution.py:236
  224.1 2.3 %collective-permute-done.22.refs_4_ = bf16[4,2,16,256]{3,2,1,0:T(8,128)(2,1)S(1)} collective-permute-done((bf16[4,2,16,256]{3,2,1,0:T(8,128)(2,1)S(1)}, bf16[4,2,16,256]{3,2,1,0:T(8,128)(2,1)S(1)}, u32[]{:S(2)}, u32[]{:S(2)}) %collective-permute-start.22) | collective-permute-done | bytes 65568 | tf_op jit(solution)/shard_map/ppermute | solution.py:236
  (40 shorter events, 11.9 us)
Async XLA Ops:
  0.6 51.4 %copy-start = (s32[64,256]{1,0:T(8,128)S(1)}, s32[64,256]{1,0:T(8,128)}, u32[]{:S(2)}) copy-start(s32[64,256]{1,0:T(8,128)} %param.12) | copy-start | bytes 196612
  1.7 2.2 copy-start.1
  3.9 1.0 copy-start.5
  4.9 40.5 %copy-start.3 = (bf16[4,1,64,2,16,256]{5,4,3,2,1,0:T(8,128)(2,1)S(1)}, bf16[4,1,64,2,16,256]{5,4,3,2,1,0:T(8,128)(2,1)}, u32[]{:S(2)}) copy-start(bf16[4,1,64,2,16,256]{5,4,3,2,1,0:T(8,128)(2,1)} %refs_1_.8) | copy-start | bytes 12582916
  6.2 45.7 %copy-start.7 = (bf16[2,448,256]{2,1,0:T(8,128)(2,1)S(1)}, bf16[2,448,256]{2,1,0:T(8,128)(2,1)}, u32[]{:S(2)}) copy-start(bf16[2,448,256]{2,1,0:T(8,128)(2,1)} %constant.21.clone) | copy-start | bytes 1376260
  6.2 45.7 %copy-start.8 = (bf16[2,256,448]{2,1,0:T(8,128)(2,1)S(1)}, bf16[2,256,448]{2,1,0:T(8,128)(2,1)}, u32[]{:S(2)}) copy-start(bf16[2,256,448]{2,1,0:T(8,128)(2,1)} %constant.20.clone) | copy-start | bytes 1376260
  46.2 5.9 %collective-permute-start = (bf16[4,2,16,256]{3,2,1,0:T(8,128)(2,1)S(1)}, bf16[4,2,16,256]{3,2,1,0:T(8,128)(2,1)S(1)}, u32[]{:S(2)}, u32[]{:S(2)}) collective-permute-start(bf16[4,2,16,256]{3,2,1,0:T(8,128)(2,1)S(1)} %get-tuple-element.48), channel_id=1, source_target_pairs={{0,64},{64,128},{128,192},{192,0},{1,65},{65,129},{129,193},{193,1... | collective-permute-start | bytes 196616 | tf_op jit(solution)/shard_map/ppermute | solution.py:236
  47.7 6.7 %collective-permute-start.1 = (bf16[4,2,16,256]{3,2,1,0:T(8,128)(2,1)S(1)}, bf16[4,2,16,256]{3,2,1,0:T(8,128)(2,1)S(1)}, u32[]{:S(2)}, u32[]{:S(2)}) collective-permute-start(bf16[4,2,16,256]{3,2,1,0:T(8,128)(2,1)S(1)} %get-tuple-element.49), channel_id=1, source_target_pairs={{0,128},{64,192},{128,0},{192,64},{1,129},{65,193},{129,1},{193,65... | collective-permute-start | bytes 196616 | tf_op jit(solution)/shard_map/ppermute | solution.py:236
  50.5 4.8 %collective-permute-start.2 = (bf16[4,2,16,256]{3,2,1,0:T(8,128)(2,1)S(1)}, bf16[4,2,16,256]{3,2,1,0:T(8,128)(2,1)S(1)}, u32[]{:S(2)}, u32[]{:S(2)}) collective-permute-start(bf16[4,2,16,256]{3,2,1,0:T(8,128)(2,1)S(1)} %get-tuple-element.50), channel_id=1, source_target_pairs={{0,192},{64,0},{128,64},{192,128},{1,193},{65,1},{129,65},{193,129... | collective-permute-start | bytes 196616 | tf_op jit(solution)/shard_map/ppermute | solution.py:236
  51.9 13.3 %copy-start.4 = (bf16[4,1,64,2,16,256]{5,4,3,2,1,0:T(8,128)(2,1)S(1)}, bf16[4,1,64,2,16,256]{5,4,3,2,1,0:T(8,128)(2,1)}, u32[]{:S(2)}) copy-start(bf16[4,1,64,2,16,256]{5,4,3,2,1,0:T(8,128)(2,1)} %refs_1_.8) | copy-start | bytes 12582916
  56.8 5.9 %collective-permute-start.3 = (bf16[4,2,16,256]{3,2,1,0:T(8,128)(2,1)S(1)}, bf16[4,2,16,256]{3,2,1,0:T(8,128)(2,1)S(1)}, u32[]{:S(2)}, u32[]{:S(2)}) collective-permute-start(bf16[4,2,16,256]{3,2,1,0:T(8,128)(2,1)S(1)} %get-tuple-element.53), channel_id=1, source_target_pairs={{0,64},{64,128},{128,192},{192,0},{1,65},{65,129},{129,193},{193,1... | collective-permute-start | bytes 196616 | tf_op jit(solution)/shard_map/ppermute | solution.py:236
  58.1 6.2 %collective-permute-start.4 = (bf16[4,2,16,256]{3,2,1,0:T(8,128)(2,1)S(1)}, bf16[4,2,16,256]{3,2,1,0:T(8,128)(2,1)S(1)}, u32[]{:S(2)}, u32[]{:S(2)}) collective-permute-start(bf16[4,2,16,256]{3,2,1,0:T(8,128)(2,1)S(1)} %get-tuple-element.54), channel_id=1, source_target_pairs={{0,128},{64,192},{128,0},{192,64},{1,129},{65,193},{129,1},{193,65... | collective-permute-start | bytes 196616 | tf_op jit(solution)/shard_map/ppermute | solution.py:236
  61.0 4.3 %collective-permute-start.5 = (bf16[4,2,16,256]{3,2,1,0:T(8,128)(2,1)S(1)}, bf16[4,2,16,256]{3,2,1,0:T(8,128)(2,1)S(1)}, u32[]{:S(2)}, u32[]{:S(2)}) collective-permute-start(bf16[4,2,16,256]{3,2,1,0:T(8,128)(2,1)S(1)} %get-tuple-element.55), channel_id=1, source_target_pairs={{0,192},{64,0},{128,64},{192,128},{1,193},{65,1},{129,65},{193,129... | collective-permute-start | bytes 196616 | tf_op jit(solution)/shard_map/ppermute | solution.py:236
  65.2 35.2 %copy-start.2 = (bf16[4,64,1,2,16,256]{5,4,3,2,1,0:T(8,128)(2,1)S(1)}, bf16[4,64,1,2,16,256]{5,4,3,2,1,0:T(8,128)(2,1)}, u32[]{:S(2)}) copy-start(bf16[4,64,1,2,16,256]{5,4,3,2,1,0:T(8,128)(2,1)} %f_ref.7) | copy-start | bytes 12582916
  100.5 19.2 %copy-start.6 = (f32[4,2,64,256]{3,2,1,0:T(8,128)S(1)}, f32[4,2,64,256]{3,2,1,0:T(8,128)}, u32[]{:S(2)}) copy-start(f32[4,2,64,256]{3,2,1,0:T(8,128)} %refs_1_.9) | copy-start | bytes 1572868
  101.2 6.2 %collective-permute-start.6 = (bf16[4,2,16,256]{3,2,1,0:T(8,128)(2,1)S(1)}, bf16[4,2,16,256]{3,2,1,0:T(8,128)(2,1)S(1)}, u32[]{:S(2)}, u32[]{:S(2)}) collective-permute-start(bf16[4,2,16,256]{3,2,1,0:T(8,128)(2,1)S(1)} %get-tuple-element.57), channel_id=1, source_target_pairs={{0,64},{64,128},{128,192},{192,0},{1,65},{65,129},{129,193},{193,1... | collective-permute-start | bytes 196616 | tf_op jit(solution)/shard_map/ppermute | solution.py:236
  101.3 7.0 %collective-permute-start.7 = (bf16[4,2,16,256]{3,2,1,0:T(8,128)(2,1)S(1)}, bf16[4,2,16,256]{3,2,1,0:T(8,128)(2,1)S(1)}, u32[]{:S(2)}, u32[]{:S(2)}) collective-permute-start(bf16[4,2,16,256]{3,2,1,0:T(8,128)(2,1)S(1)} %get-tuple-element.58), channel_id=1, source_target_pairs={{0,128},{64,192},{128,0},{192,64},{1,129},{65,193},{129,1},{193,65... | collective-permute-start | bytes 196616 | tf_op jit(solution)/shard_map/ppermute | solution.py:236
  104.2 5.4 %collective-permute-start.8 = (bf16[4,2,16,256]{3,2,1,0:T(8,128)(2,1)S(1)}, bf16[4,2,16,256]{3,2,1,0:T(8,128)(2,1)S(1)}, u32[]{:S(2)}, u32[]{:S(2)}) collective-permute-start(bf16[4,2,16,256]{3,2,1,0:T(8,128)(2,1)S(1)} %get-tuple-element.59), channel_id=1, source_target_pairs={{0,192},{64,0},{128,64},{192,128},{1,193},{65,1},{129,65},{193,129... | collective-permute-start | bytes 196616 | tf_op jit(solution)/shard_map/ppermute | solution.py:236
  111.1 5.6 %collective-permute-start.9 = (bf16[4,2,16,256]{3,2,1,0:T(8,128)(2,1)S(1)}, bf16[4,2,16,256]{3,2,1,0:T(8,128)(2,1)S(1)}, u32[]{:S(2)}, u32[]{:S(2)}) collective-permute-start(bf16[4,2,16,256]{3,2,1,0:T(8,128)(2,1)S(1)} %get-tuple-element.61), channel_id=1, source_target_pairs={{0,64},{64,128},{128,192},{192,0},{1,65},{65,129},{129,193},{193,1... | collective-permute-start | bytes 196616 | tf_op jit(solution)/shard_map/ppermute | solution.py:236
  112.2 6.7 %collective-permute-start.10 = (bf16[4,2,16,256]{3,2,1,0:T(8,128)(2,1)S(1)}, bf16[4,2,16,256]{3,2,1,0:T(8,128)(2,1)S(1)}, u32[]{:S(2)}, u32[]{:S(2)}) collective-permute-start(bf16[4,2,16,256]{3,2,1,0:T(8,128)(2,1)S(1)} %get-tuple-element.62), channel_id=1, source_target_pairs={{0,128},{64,192},{128,0},{192,64},{1,129},{65,193},{129,1},{193,65... | collective-permute-start | bytes 196616 | tf_op jit(solution)/shard_map/ppermute | solution.py:236
  115.4 4.3 %collective-permute-start.11 = (bf16[4,2,16,256]{3,2,1,0:T(8,128)(2,1)S(1)}, bf16[4,2,16,256]{3,2,1,0:T(8,128)(2,1)S(1)}, u32[]{:S(2)}, u32[]{:S(2)}) collective-permute-start(bf16[4,2,16,256]{3,2,1,0:T(8,128)(2,1)S(1)} %get-tuple-element.63), channel_id=1, source_target_pairs={{0,192},{64,0},{128,64},{192,128},{1,193},{65,1},{129,65},{193,129... | collective-permute-start | bytes 196616 | tf_op jit(solution)/shard_map/ppermute | solution.py:236
  155.0 6.2 %collective-permute-start.12 = (bf16[4,2,16,256]{3,2,1,0:T(8,128)(2,1)S(1)}, bf16[4,2,16,256]{3,2,1,0:T(8,128)(2,1)S(1)}, u32[]{:S(2)}, u32[]{:S(2)}) collective-permute-start(bf16[4,2,16,256]{3,2,1,0:T(8,128)(2,1)S(1)} %get-tuple-element.65), channel_id=1, source_target_pairs={{0,64},{64,128},{128,192},{192,0},{1,65},{65,129},{129,193},{193,1... | collective-permute-start | bytes 196616 | tf_op jit(solution)/shard_map/ppermute | solution.py:236
  155.1 7.0 %collective-permute-start.13 = (bf16[4,2,16,256]{3,2,1,0:T(8,128)(2,1)S(1)}, bf16[4,2,16,256]{3,2,1,0:T(8,128)(2,1)S(1)}, u32[]{:S(2)}, u32[]{:S(2)}) collective-permute-start(bf16[4,2,16,256]{3,2,1,0:T(8,128)(2,1)S(1)} %get-tuple-element.66), channel_id=1, source_target_pairs={{0,128},{64,192},{128,0},{192,64},{1,129},{65,193},{129,1},{193,65... | collective-permute-start | bytes 196616 | tf_op jit(solution)/shard_map/ppermute | solution.py:236
  158.0 5.4 %collective-permute-start.14 = (bf16[4,2,16,256]{3,2,1,0:T(8,128)(2,1)S(1)}, bf16[4,2,16,256]{3,2,1,0:T(8,128)(2,1)S(1)}, u32[]{:S(2)}, u32[]{:S(2)}) collective-permute-start(bf16[4,2,16,256]{3,2,1,0:T(8,128)(2,1)S(1)} %get-tuple-element.67), channel_id=1, source_target_pairs={{0,192},{64,0},{128,64},{192,128},{1,193},{65,1},{129,65},{193,129... | collective-permute-start | bytes 196616 | tf_op jit(solution)/shard_map/ppermute | solution.py:236
  164.8 5.6 %collective-permute-start.15 = (bf16[4,2,16,256]{3,2,1,0:T(8,128)(2,1)S(1)}, bf16[4,2,16,256]{3,2,1,0:T(8,128)(2,1)S(1)}, u32[]{:S(2)}, u32[]{:S(2)}) collective-permute-start(bf16[4,2,16,256]{3,2,1,0:T(8,128)(2,1)S(1)} %get-tuple-element.69), channel_id=1, source_target_pairs={{0,64},{64,128},{128,192},{192,0},{1,65},{65,129},{129,193},{193,1... | collective-permute-start | bytes 196616 | tf_op jit(solution)/shard_map/ppermute | solution.py:236
  166.0 6.7 %collective-permute-start.16 = (bf16[4,2,16,256]{3,2,1,0:T(8,128)(2,1)S(1)}, bf16[4,2,16,256]{3,2,1,0:T(8,128)(2,1)S(1)}, u32[]{:S(2)}, u32[]{:S(2)}) collective-permute-start(bf16[4,2,16,256]{3,2,1,0:T(8,128)(2,1)S(1)} %get-tuple-element.70), channel_id=1, source_target_pairs={{0,128},{64,192},{128,0},{192,64},{1,129},{65,193},{129,1},{193,65... | collective-permute-start | bytes 196616 | tf_op jit(solution)/shard_map/ppermute | solution.py:236
  169.2 4.3 %collective-permute-start.17 = (bf16[4,2,16,256]{3,2,1,0:T(8,128)(2,1)S(1)}, bf16[4,2,16,256]{3,2,1,0:T(8,128)(2,1)S(1)}, u32[]{:S(2)}, u32[]{:S(2)}) collective-permute-start(bf16[4,2,16,256]{3,2,1,0:T(8,128)(2,1)S(1)} %get-tuple-element.71), channel_id=1, source_target_pairs={{0,192},{64,0},{128,64},{192,128},{1,193},{65,1},{129,65},{193,129... | collective-permute-start | bytes 196616 | tf_op jit(solution)/shard_map/ppermute | solution.py:236
  208.7 6.2 %collective-permute-start.18 = (bf16[4,2,16,256]{3,2,1,0:T(8,128)(2,1)S(1)}, bf16[4,2,16,256]{3,2,1,0:T(8,128)(2,1)S(1)}, u32[]{:S(2)}, u32[]{:S(2)}) collective-permute-start(bf16[4,2,16,256]{3,2,1,0:T(8,128)(2,1)S(1)} %get-tuple-element.73), channel_id=1, source_target_pairs={{0,64},{64,128},{128,192},{192,0},{1,65},{65,129},{129,193},{193,1... | collective-permute-start | bytes 196616 | tf_op jit(solution)/shard_map/ppermute | solution.py:236
  208.8 7.0 %collective-permute-start.19 = (bf16[4,2,16,256]{3,2,1,0:T(8,128)(2,1)S(1)}, bf16[4,2,16,256]{3,2,1,0:T(8,128)(2,1)S(1)}, u32[]{:S(2)}, u32[]{:S(2)}) collective-permute-start(bf16[4,2,16,256]{3,2,1,0:T(8,128)(2,1)S(1)} %get-tuple-element.74), channel_id=1, source_target_pairs={{0,128},{64,192},{128,0},{192,64},{1,129},{65,193},{129,1},{193,65... | collective-permute-start | bytes 196616 | tf_op jit(solution)/shard_map/ppermute | solution.py:236
  211.7 5.4 %collective-permute-start.20 = (bf16[4,2,16,256]{3,2,1,0:T(8,128)(2,1)S(1)}, bf16[4,2,16,256]{3,2,1,0:T(8,128)(2,1)S(1)}, u32[]{:S(2)}, u32[]{:S(2)}) collective-permute-start(bf16[4,2,16,256]{3,2,1,0:T(8,128)(2,1)S(1)} %get-tuple-element.75), channel_id=1, source_target_pairs={{0,192},{64,0},{128,64},{192,128},{1,193},{65,1},{129,65},{193,129... | collective-permute-start | bytes 196616 | tf_op jit(solution)/shard_map/ppermute | solution.py:236
  218.6 5.6 %collective-permute-start.21 = (bf16[4,2,16,256]{3,2,1,0:T(8,128)(2,1)S(1)}, bf16[4,2,16,256]{3,2,1,0:T(8,128)(2,1)S(1)}, u32[]{:S(2)}, u32[]{:S(2)}) collective-permute-start(bf16[4,2,16,256]{3,2,1,0:T(8,128)(2,1)S(1)} %get-tuple-element.77), channel_id=1, source_target_pairs={{0,64},{64,128},{128,192},{192,0},{1,65},{65,129},{129,193},{193,1... | collective-permute-start | bytes 196616 | tf_op jit(solution)/shard_map/ppermute | solution.py:236
  219.7 6.7 %collective-permute-start.22 = (bf16[4,2,16,256]{3,2,1,0:T(8,128)(2,1)S(1)}, bf16[4,2,16,256]{3,2,1,0:T(8,128)(2,1)S(1)}, u32[]{:S(2)}, u32[]{:S(2)}) collective-permute-start(bf16[4,2,16,256]{3,2,1,0:T(8,128)(2,1)S(1)} %get-tuple-element.78), channel_id=1, source_target_pairs={{0,128},{64,192},{128,0},{192,64},{1,129},{65,193},{129,1},{193,65... | collective-permute-start | bytes 196616 | tf_op jit(solution)/shard_map/ppermute | solution.py:236
  222.9 4.3 %collective-permute-start.23 = (bf16[4,2,16,256]{3,2,1,0:T(8,128)(2,1)S(1)}, bf16[4,2,16,256]{3,2,1,0:T(8,128)(2,1)S(1)}, u32[]{:S(2)}, u32[]{:S(2)}) collective-permute-start(bf16[4,2,16,256]{3,2,1,0:T(8,128)(2,1)S(1)} %get-tuple-element.79), channel_id=1, source_target_pairs={{0,192},{64,0},{128,64},{192,128},{1,193},{65,1},{129,65},{193,129... | collective-permute-start | bytes 196616 | tf_op jit(solution)/shard_map/ppermute | solution.py:236

commit v4 on v3

--- a/solution.py
+++ b/solution.py
@@ -91,10 +91,12 @@
     for f in range(OWN):
         z = z_ref[:, f] * mask_ref[f] if forward else z_ref[:, f]
         z = z.reshape(TILES * RMAX, 2 * FOCAL)
-        straight, crossed = [
-            dot_tn(z, (f_ref[f, 0, :, c] if forward else f_ref[f, :, 0, c]).reshape(TILES * RMAX, TILE))
+        sides = [
+            (f_ref[f, 0, :, c] if forward else f_ref[f, :, 0, c]).reshape(TILES * RMAX, TILE)
             for c in range(2)
         ]
+        both = dot_tn(z, jnp.concatenate(sides, axis=1))
+        straight, crossed = both[:, :TILE], both[:, TILE:]
         for r in range(GROUPS):
             for g in range(SETS):
                 at = (r * SETS + g) * 2 * PW

time: 228 us -> 228 us (level)
  no operation moved by 1% of the time
where the time goes in v4:
time: 228 us
  blocking collectives  140 us (61%)
  starting transfers between devices  36.5 us (16%)
  waiting for transfers between devices  30.3 us (13%)
  Pallas kernels  15.6 us (7%)
  local copies, waits for them, and re-layouts  4.14 us (2%)
    all_to_all x4, blocking collectives, route(): lax.all_to_all(z.reshape(TILES, OWN * RMAX, 2 * FOCAL), 'tile', 0, 0, til...  140 us
    ppermute x24, starting transfers between devices, exchange(): lax.ppermute(parts[r], 'freq', [(i, (i + r) % GROUPS) for i in range(GROU...  36.5 us
    ppermute x24, waiting for transfers between devices, exchange(): lax.ppermute(parts[r], 'freq', [(i, (i + r) % GROUPS) for i in range(GROU...  30.3 us
    pallas_call x4, Pallas kernels, window(): pl.pallas_call(window_kernel, in_specs=vmem(GROUPS + 3), out_specs=vmem(G...  5.85 us
    pallas_call x4, Pallas kernels, project(): pl.pallas_call(functools.partial(project_kernel, forward, len(field) > 0)...  5.03 us
  transfers between devices with their start and end apart: 24, of which 23 were waited for; matrix products, arithmetic and copies ran while one was open for 0% of the time, Pallas kernels for 0%

profile of v4, /device:TPU:8, one launch (start us, length us, event | category | flops | bytes accessed | tf_op | source)
XLA Modules:
  0.0 228.1 jit_solution(4375745055657161986)
XLA Ops:
  0.6 1.0 fusion.outs_0_.refs_0_
  1.7 2.2 copy-done.1
  3.9 1.0 copy-done.5
  4.9 1.2 project.4
  6.2 39.2 %all_to_all.20 = bf16[64,64,128]{2,1,0:T(8,128)(2,1)S(1)} all-to-all(bf16[64,64,128]{2,1,0:T(8,128)(2,1)S(1)} %bitcast.17), channel_id=1, replica_groups=mesh['freq'=4,'tile'=64] {'tile'}, dimensions={0} | all-to-all | bytes 2097152 | tf_op jit(solution)/shard_map/all_to_all | solution.py:249
  46.2 1.6 collective-permute-start
  47.7 2.7 %collective-permute-start.1 = (bf16[4,2,16,256]{3,2,1,0:T(8,128)(2,1)S(1)}, bf16[4,2,16,256]{3,2,1,0:T(8,128)(2,1)S(1)}, u32[]{:S(2)}, u32[]{:S(2)}) collective-permute-start(bf16[4,2,16,256]{3,2,1,0:T(8,128)(2,1)S(1)} %get-tuple-element.49), channel_id=1, source_target_pairs={{0,128},{64,192},{128,0},{192,64},{1,129},{65,193},{129,1},{193,65... | collective-permute-start | bytes 196616 | tf_op jit(solution)/shard_map/ppermute | solution.py:238
  50.5 1.4 collective-permute-start.2
  52.1 2.3 %collective-permute-done.1.s2 = bf16[4,2,16,256]{3,2,1,0:T(8,128)(2,1)S(1)} collective-permute-done((bf16[4,2,16,256]{3,2,1,0:T(8,128)(2,1)S(1)}, bf16[4,2,16,256]{3,2,1,0:T(8,128)(2,1)S(1)}, u32[]{:S(2)}, u32[]{:S(2)}) %collective-permute-start.1) | collective-permute-done | bytes 65568 | tf_op jit(solution)/shard_map/ppermute | solution.py:238
  54.4 0.9 collective-permute-done.2.s3
  55.3 1.5 window.4
  56.8 1.4 collective-permute-start.3
  58.1 2.8 %collective-permute-start.4 = (bf16[4,2,16,256]{3,2,1,0:T(8,128)(2,1)S(1)}, bf16[4,2,16,256]{3,2,1,0:T(8,128)(2,1)S(1)}, u32[]{:S(2)}, u32[]{:S(2)}) collective-permute-start(bf16[4,2,16,256]{3,2,1,0:T(8,128)(2,1)S(1)} %get-tuple-element.54), channel_id=1, source_target_pairs={{0,128},{64,192},{128,0},{192,64},{1,129},{65,193},{129,1},{193,65... | collective-permute-start | bytes 196616 | tf_op jit(solution)/shard_map/ppermute | solution.py:238
  61.8 0.9 collective-permute-done.3.refs_3_
  62.6 1.7 collective-permute-done.4.refs_4_
  64.3 0.9 collective-permute-done.5.refs_5_
  65.2 1.3 project.5
  66.5 34.0 %all_to_all.21 = bf16[64,64,128]{2,1,0:T(8,128)(2,1)S(1)} all-to-all(bf16[64,64,128]{2,1,0:T(8,128)(2,1)S(1)} %bitcast.14), channel_id=1, replica_groups=mesh['freq'=4,'tile'=64] {'tile'}, dimensions={0} | all-to-all | bytes 2097152 | tf_op jit(solution)/shard_map/all_to_all | solution.py:249
  101.3 2.9 %collective-permute-start.7 = (bf16[4,2,16,256]{3,2,1,0:T(8,128)(2,1)S(1)}, bf16[4,2,16,256]{3,2,1,0:T(8,128)(2,1)S(1)}, u32[]{:S(2)}, u32[]{:S(2)}) collective-permute-start(bf16[4,2,16,256]{3,2,1,0:T(8,128)(2,1)S(1)} %get-tuple-element.58), channel_id=1, source_target_pairs={{0,128},{64,192},{128,0},{192,64},{1,129},{65,193},{129,1},{193,65... | collective-permute-start | bytes 196616 | tf_op jit(solution)/shard_map/ppermute | solution.py:238
  104.2 1.2 collective-permute-start.8
  106.2 1.3 collective-permute-done.6.s1
  108.3 1.3 collective-permute-done.8.s3
  109.6 1.5 window.5
  111.1 1.1 collective-permute-start.9
  112.2 3.2 %collective-permute-start.10 = (bf16[4,2,16,256]{3,2,1,0:T(8,128)(2,1)S(1)}, bf16[4,2,16,256]{3,2,1,0:T(8,128)(2,1)S(1)}, u32[]{:S(2)}, u32[]{:S(2)}) collective-permute-start(bf16[4,2,16,256]{3,2,1,0:T(8,128)(2,1)S(1)} %get-tuple-element.62), channel_id=1, source_target_pairs={{0,128},{64,192},{128,0},{192,64},{1,129},{65,193},{129,1},{193,65... | collective-permute-start | bytes 196616 | tf_op jit(solution)/shard_map/ppermute | solution.py:238
  115.4 1.2 collective-permute-done.9.refs_3_
  116.6 2.3 %collective-permute-done.10.refs_4_ = bf16[4,2,16,256]{3,2,1,0:T(8,128)(2,1)S(1)} collective-permute-done((bf16[4,2,16,256]{3,2,1,0:T(8,128)(2,1)S(1)}, bf16[4,2,16,256]{3,2,1,0:T(8,128)(2,1)S(1)}, u32[]{:S(2)}, u32[]{:S(2)}) %collective-permute-start.10) | collective-permute-done | bytes 65568 | tf_op jit(solution)/shard_map/ppermute | solution.py:238
  119.7 1.3 project.6
  121.0 33.2 %all_to_all.22 = bf16[64,64,128]{2,1,0:T(8,128)(2,1)S(1)} all-to-all(bf16[64,64,128]{2,1,0:T(8,128)(2,1)S(1)} %bitcast.15), channel_id=1, replica_groups=mesh['freq'=4,'tile'=64] {'tile'}, dimensions={0} | all-to-all | bytes 2097152 | tf_op jit(solution)/shard_map/all_to_all | solution.py:249
  155.1 2.9 %collective-permute-start.13 = (bf16[4,2,16,256]{3,2,1,0:T(8,128)(2,1)S(1)}, bf16[4,2,16,256]{3,2,1,0:T(8,128)(2,1)S(1)}, u32[]{:S(2)}, u32[]{:S(2)}) collective-permute-start(bf16[4,2,16,256]{3,2,1,0:T(8,128)(2,1)S(1)} %get-tuple-element.66), channel_id=1, source_target_pairs={{0,128},{64,192},{128,0},{192,64},{1,129},{65,193},{129,1},{193,65... | collective-permute-start | bytes 196616 | tf_op jit(solution)/shard_map/ppermute | solution.py:238
  158.0 1.3 collective-permute-start.14
  159.2 2.0 collective-permute-done.12.s1
  162.1 1.3 collective-permute-done.14.s3
  163.4 1.5 window.6
  164.8 1.1 collective-permute-start.15
  166.0 3.2 %collective-permute-start.16 = (bf16[4,2,16,256]{3,2,1,0:T(8,128)(2,1)S(1)}, bf16[4,2,16,256]{3,2,1,0:T(8,128)(2,1)S(1)}, u32[]{:S(2)}, u32[]{:S(2)}) collective-permute-start(bf16[4,2,16,256]{3,2,1,0:T(8,128)(2,1)S(1)} %get-tuple-element.70), channel_id=1, source_target_pairs={{0,128},{64,192},{128,0},{192,64},{1,129},{65,193},{129,1},{193,65... | collective-permute-start | bytes 196616 | tf_op jit(solution)/shard_map/ppermute | solution.py:238
  169.2 1.2 collective-permute-done.15.refs_3_.refs_2_
  170.4 2.3 %collective-permute-done.16.refs_4_.refs_3_ = bf16[4,2,16,256]{3,2,1,0:T(8,128)(2,1)S(1)} collective-permute-done((bf16[4,2,16,256]{3,2,1,0:T(8,128)(2,1)S(1)}, bf16[4,2,16,256]{3,2,1,0:T(8,128)(2,1)S(1)}, u32[]{:S(2)}, u32[]{:S(2)}) %collective-permute-start.16) | collective-permute-done | bytes 65568 | tf_op jit(solution)/shard_map/ppermute | solution.py:238
  173.5 1.3 project.7
  174.7 33.2 %all_to_all.23 = bf16[64,64,128]{2,1,0:T(8,128)(2,1)S(1)} all-to-all(bf16[64,64,128]{2,1,0:T(8,128)(2,1)S(1)} %bitcast.16), channel_id=1, replica_groups=mesh['freq'=4,'tile'=64] {'tile'}, dimensions={0} | all-to-all | bytes 2097152 | tf_op jit(solution)/shard_map/all_to_all | solution.py:249
  208.8 2.9 %collective-permute-start.19 = (bf16[4,2,16,256]{3,2,1,0:T(8,128)(2,1)S(1)}, bf16[4,2,16,256]{3,2,1,0:T(8,128)(2,1)S(1)}, u32[]{:S(2)}, u32[]{:S(2)}) collective-permute-start(bf16[4,2,16,256]{3,2,1,0:T(8,128)(2,1)S(1)} %get-tuple-element.74), channel_id=1, source_target_pairs={{0,128},{64,192},{128,0},{192,64},{1,129},{65,193},{129,1},{193,65... | collective-permute-start | bytes 196616 | tf_op jit(solution)/shard_map/ppermute | solution.py:238
  211.7 1.3 collective-permute-start.20
  212.9 2.0 collective-permute-done.18.s1
  215.8 1.3 collective-permute-done.20.s3
  217.1 1.5 window.7
  218.6 1.1 collective-permute-start.21
  219.7 3.2 %collective-permute-start.22 = (bf16[4,2,16,256]{3,2,1,0:T(8,128)(2,1)S(1)}, bf16[4,2,16,256]{3,2,1,0:T(8,128)(2,1)S(1)}, u32[]{:S(2)}, u32[]{:S(2)}) collective-permute-start(bf16[4,2,16,256]{3,2,1,0:T(8,128)(2,1)S(1)} %get-tuple-element.78), channel_id=1, source_target_pairs={{0,128},{64,192},{128,0},{192,64},{1,129},{65,193},{129,1},{193,65... | collective-permute-start | bytes 196616 | tf_op jit(solution)/shard_map/ppermute | solution.py:238
  224.1 2.3 %collective-permute-done.22.refs_4_ = bf16[4,2,16,256]{3,2,1,0:T(8,128)(2,1)S(1)} collective-permute-done((bf16[4,2,16,256]{3,2,1,0:T(8,128)(2,1)S(1)}, bf16[4,2,16,256]{3,2,1,0:T(8,128)(2,1)S(1)}, u32[]{:S(2)}, u32[]{:S(2)}) %collective-permute-start.22) | collective-permute-done | bytes 65568 | tf_op jit(solution)/shard_map/ppermute | solution.py:238
  (40 shorter events, 11.9 us)
Async XLA Ops:
  0.6 51.4 %copy-start = (s32[64,256]{1,0:T(8,128)S(1)}, s32[64,256]{1,0:T(8,128)}, u32[]{:S(2)}) copy-start(s32[64,256]{1,0:T(8,128)} %param.12) | copy-start | bytes 196612
  1.7 2.2 copy-start.1
  3.9 1.0 copy-start.5
  4.9 40.5 %copy-start.3 = (bf16[4,1,64,2,16,256]{5,4,3,2,1,0:T(8,128)(2,1)S(1)}, bf16[4,1,64,2,16,256]{5,4,3,2,1,0:T(8,128)(2,1)}, u32[]{:S(2)}) copy-start(bf16[4,1,64,2,16,256]{5,4,3,2,1,0:T(8,128)(2,1)} %refs_1_.8) | copy-start | bytes 12582916
  6.2 45.7 %copy-start.7 = (bf16[2,448,256]{2,1,0:T(8,128)(2,1)S(1)}, bf16[2,448,256]{2,1,0:T(8,128)(2,1)}, u32[]{:S(2)}) copy-start(bf16[2,448,256]{2,1,0:T(8,128)(2,1)} %constant.21.clone) | copy-start | bytes 1376260
  6.2 45.7 %copy-start.8 = (bf16[2,256,448]{2,1,0:T(8,128)(2,1)S(1)}, bf16[2,256,448]{2,1,0:T(8,128)(2,1)}, u32[]{:S(2)}) copy-start(bf16[2,256,448]{2,1,0:T(8,128)(2,1)} %constant.20.clone) | copy-start | bytes 1376260
  46.2 5.9 %collective-permute-start = (bf16[4,2,16,256]{3,2,1,0:T(8,128)(2,1)S(1)}, bf16[4,2,16,256]{3,2,1,0:T(8,128)(2,1)S(1)}, u32[]{:S(2)}, u32[]{:S(2)}) collective-permute-start(bf16[4,2,16,256]{3,2,1,0:T(8,128)(2,1)S(1)} %get-tuple-element.48), channel_id=1, source_target_pairs={{0,64},{64,128},{128,192},{192,0},{1,65},{65,129},{129,193},{193,1... | collective-permute-start | bytes 196616 | tf_op jit(solution)/shard_map/ppermute | solution.py:238
  47.7 6.7 %collective-permute-start.1 = (bf16[4,2,16,256]{3,2,1,0:T(8,128)(2,1)S(1)}, bf16[4,2,16,256]{3,2,1,0:T(8,128)(2,1)S(1)}, u32[]{:S(2)}, u32[]{:S(2)}) collective-permute-start(bf16[4,2,16,256]{3,2,1,0:T(8,128)(2,1)S(1)} %get-tuple-element.49), channel_id=1, source_target_pairs={{0,128},{64,192},{128,0},{192,64},{1,129},{65,193},{129,1},{193,65... | collective-permute-start | bytes 196616 | tf_op jit(solution)/shard_map/ppermute | solution.py:238
  50.5 4.8 %collective-permute-start.2 = (bf16[4,2,16,256]{3,2,1,0:T(8,128)(2,1)S(1)}, bf16[4,2,16,256]{3,2,1,0:T(8,128)(2,1)S(1)}, u32[]{:S(2)}, u32[]{:S(2)}) collective-permute-start(bf16[4,2,16,256]{3,2,1,0:T(8,128)(2,1)S(1)} %get-tuple-element.50), channel_id=1, source_target_pairs={{0,192},{64,0},{128,64},{192,128},{1,193},{65,1},{129,65},{193,129... | collective-permute-start | bytes 196616 | tf_op jit(solution)/shard_map/ppermute | solution.py:238
  51.9 13.3 %copy-start.4 = (bf16[4,1,64,2,16,256]{5,4,3,2,1,0:T(8,128)(2,1)S(1)}, bf16[4,1,64,2,16,256]{5,4,3,2,1,0:T(8,128)(2,1)}, u32[]{:S(2)}) copy-start(bf16[4,1,64,2,16,256]{5,4,3,2,1,0:T(8,128)(2,1)} %refs_1_.8) | copy-start | bytes 12582916
  56.8 5.9 %collective-permute-start.3 = (bf16[4,2,16,256]{3,2,1,0:T(8,128)(2,1)S(1)}, bf16[4,2,16,256]{3,2,1,0:T(8,128)(2,1)S(1)}, u32[]{:S(2)}, u32[]{:S(2)}) collective-permute-start(bf16[4,2,16,256]{3,2,1,0:T(8,128)(2,1)S(1)} %get-tuple-element.53), channel_id=1, source_target_pairs={{0,64},{64,128},{128,192},{192,0},{1,65},{65,129},{129,193},{193,1... | collective-permute-start | bytes 196616 | tf_op jit(solution)/shard_map/ppermute | solution.py:238
  58.1 6.2 %collective-permute-start.4 = (bf16[4,2,16,256]{3,2,1,0:T(8,128)(2,1)S(1)}, bf16[4,2,16,256]{3,2,1,0:T(8,128)(2,1)S(1)}, u32[]{:S(2)}, u32[]{:S(2)}) collective-permute-start(bf16[4,2,16,256]{3,2,1,0:T(8,128)(2,1)S(1)} %get-tuple-element.54), channel_id=1, source_target_pairs={{0,128},{64,192},{128,0},{192,64},{1,129},{65,193},{129,1},{193,65... | collective-permute-start | bytes 196616 | tf_op jit(solution)/shard_map/ppermute | solution.py:238
  61.0 4.3 %collective-permute-start.5 = (bf16[4,2,16,256]{3,2,1,0:T(8,128)(2,1)S(1)}, bf16[4,2,16,256]{3,2,1,0:T(8,128)(2,1)S(1)}, u32[]{:S(2)}, u32[]{:S(2)}) collective-permute-start(bf16[4,2,16,256]{3,2,1,0:T(8,128)(2,1)S(1)} %get-tuple-element.55), channel_id=1, source_target_pairs={{0,192},{64,0},{128,64},{192,128},{1,193},{65,1},{129,65},{193,129... | collective-permute-start | bytes 196616 | tf_op jit(solution)/shard_map/ppermute | solution.py:238
  65.2 35.2 %copy-start.2 = (bf16[4,64,1,2,16,256]{5,4,3,2,1,0:T(8,128)(2,1)S(1)}, bf16[4,64,1,2,16,256]{5,4,3,2,1,0:T(8,128)(2,1)}, u32[]{:S(2)}) copy-start(bf16[4,64,1,2,16,256]{5,4,3,2,1,0:T(8,128)(2,1)} %f_ref.7) | copy-start | bytes 12582916
  100.5 19.2 %copy-start.6 = (f32[4,2,64,256]{3,2,1,0:T(8,128)S(1)}, f32[4,2,64,256]{3,2,1,0:T(8,128)}, u32[]{:S(2)}) copy-start(f32[4,2,64,256]{3,2,1,0:T(8,128)} %refs_1_.9) | copy-start | bytes 1572868
  101.2 6.2 %collective-permute-start.6 = (bf16[4,2,16,256]{3,2,1,0:T(8,128)(2,1)S(1)}, bf16[4,2,16,256]{3,2,1,0:T(8,128)(2,1)S(1)}, u32[]{:S(2)}, u32[]{:S(2)}) collective-permute-start(bf16[4,2,16,256]{3,2,1,0:T(8,128)(2,1)S(1)} %get-tuple-element.57), channel_id=1, source_target_pairs={{0,64},{64,128},{128,192},{192,0},{1,65},{65,129},{129,193},{193,1... | collective-permute-start | bytes 196616 | tf_op jit(solution)/shard_map/ppermute | solution.py:238
  101.3 7.0 %collective-permute-start.7 = (bf16[4,2,16,256]{3,2,1,0:T(8,128)(2,1)S(1)}, bf16[4,2,16,256]{3,2,1,0:T(8,128)(2,1)S(1)}, u32[]{:S(2)}, u32[]{:S(2)}) collective-permute-start(bf16[4,2,16,256]{3,2,1,0:T(8,128)(2,1)S(1)} %get-tuple-element.58), channel_id=1, source_target_pairs={{0,128},{64,192},{128,0},{192,64},{1,129},{65,193},{129,1},{193,65... | collective-permute-start | bytes 196616 | tf_op jit(solution)/shard_map/ppermute | solution.py:238
  104.2 5.4 %collective-permute-start.8 = (bf16[4,2,16,256]{3,2,1,0:T(8,128)(2,1)S(1)}, bf16[4,2,16,256]{3,2,1,0:T(8,128)(2,1)S(1)}, u32[]{:S(2)}, u32[]{:S(2)}) collective-permute-start(bf16[4,2,16,256]{3,2,1,0:T(8,128)(2,1)S(1)} %get-tuple-element.59), channel_id=1, source_target_pairs={{0,192},{64,0},{128,64},{192,128},{1,193},{65,1},{129,65},{193,129... | collective-permute-start | bytes 196616 | tf_op jit(solution)/shard_map/ppermute | solution.py:238
  111.1 5.6 %collective-permute-start.9 = (bf16[4,2,16,256]{3,2,1,0:T(8,128)(2,1)S(1)}, bf16[4,2,16,256]{3,2,1,0:T(8,128)(2,1)S(1)}, u32[]{:S(2)}, u32[]{:S(2)}) collective-permute-start(bf16[4,2,16,256]{3,2,1,0:T(8,128)(2,1)S(1)} %get-tuple-element.61), channel_id=1, source_target_pairs={{0,64},{64,128},{128,192},{192,0},{1,65},{65,129},{129,193},{193,1... | collective-permute-start | bytes 196616 | tf_op jit(solution)/shard_map/ppermute | solution.py:238
  112.2 6.7 %collective-permute-start.10 = (bf16[4,2,16,256]{3,2,1,0:T(8,128)(2,1)S(1)}, bf16[4,2,16,256]{3,2,1,0:T(8,128)(2,1)S(1)}, u32[]{:S(2)}, u32[]{:S(2)}) collective-permute-start(bf16[4,2,16,256]{3,2,1,0:T(8,128)(2,1)S(1)} %get-tuple-element.62), channel_id=1, source_target_pairs={{0,128},{64,192},{128,0},{192,64},{1,129},{65,193},{129,1},{193,65... | collective-permute-start | bytes 196616 | tf_op jit(solution)/shard_map/ppermute | solution.py:238
  115.4 4.3 %collective-permute-start.11 = (bf16[4,2,16,256]{3,2,1,0:T(8,128)(2,1)S(1)}, bf16[4,2,16,256]{3,2,1,0:T(8,128)(2,1)S(1)}, u32[]{:S(2)}, u32[]{:S(2)}) collective-permute-start(bf16[4,2,16,256]{3,2,1,0:T(8,128)(2,1)S(1)} %get-tuple-element.63), channel_id=1, source_target_pairs={{0,192},{64,0},{128,64},{192,128},{1,193},{65,1},{129,65},{193,129... | collective-permute-start | bytes 196616 | tf_op jit(solution)/shard_map/ppermute | solution.py:238
  155.0 6.2 %collective-permute-start.12 = (bf16[4,2,16,256]{3,2,1,0:T(8,128)(2,1)S(1)}, bf16[4,2,16,256]{3,2,1,0:T(8,128)(2,1)S(1)}, u32[]{:S(2)}, u32[]{:S(2)}) collective-permute-start(bf16[4,2,16,256]{3,2,1,0:T(8,128)(2,1)S(1)} %get-tuple-element.65), channel_id=1, source_target_pairs={{0,64},{64,128},{128,192},{192,0},{1,65},{65,129},{129,193},{193,1... | collective-permute-start | bytes 196616 | tf_op jit(solution)/shard_map/ppermute | solution.py:238
  155.1 7.0 %collective-permute-start.13 = (bf16[4,2,16,256]{3,2,1,0:T(8,128)(2,1)S(1)}, bf16[4,2,16,256]{3,2,1,0:T(8,128)(2,1)S(1)}, u32[]{:S(2)}, u32[]{:S(2)}) collective-permute-start(bf16[4,2,16,256]{3,2,1,0:T(8,128)(2,1)S(1)} %get-tuple-element.66), channel_id=1, source_target_pairs={{0,128},{64,192},{128,0},{192,64},{1,129},{65,193},{129,1},{193,65... | collective-permute-start | bytes 196616 | tf_op jit(solution)/shard_map/ppermute | solution.py:238
  158.0 5.4 %collective-permute-start.14 = (bf16[4,2,16,256]{3,2,1,0:T(8,128)(2,1)S(1)}, bf16[4,2,16,256]{3,2,1,0:T(8,128)(2,1)S(1)}, u32[]{:S(2)}, u32[]{:S(2)}) collective-permute-start(bf16[4,2,16,256]{3,2,1,0:T(8,128)(2,1)S(1)} %get-tuple-element.67), channel_id=1, source_target_pairs={{0,192},{64,0},{128,64},{192,128},{1,193},{65,1},{129,65},{193,129... | collective-permute-start | bytes 196616 | tf_op jit(solution)/shard_map/ppermute | solution.py:238
  164.8 5.6 %collective-permute-start.15 = (bf16[4,2,16,256]{3,2,1,0:T(8,128)(2,1)S(1)}, bf16[4,2,16,256]{3,2,1,0:T(8,128)(2,1)S(1)}, u32[]{:S(2)}, u32[]{:S(2)}) collective-permute-start(bf16[4,2,16,256]{3,2,1,0:T(8,128)(2,1)S(1)} %get-tuple-element.69), channel_id=1, source_target_pairs={{0,64},{64,128},{128,192},{192,0},{1,65},{65,129},{129,193},{193,1... | collective-permute-start | bytes 196616 | tf_op jit(solution)/shard_map/ppermute | solution.py:238
  166.0 6.7 %collective-permute-start.16 = (bf16[4,2,16,256]{3,2,1,0:T(8,128)(2,1)S(1)}, bf16[4,2,16,256]{3,2,1,0:T(8,128)(2,1)S(1)}, u32[]{:S(2)}, u32[]{:S(2)}) collective-permute-start(bf16[4,2,16,256]{3,2,1,0:T(8,128)(2,1)S(1)} %get-tuple-element.70), channel_id=1, source_target_pairs={{0,128},{64,192},{128,0},{192,64},{1,129},{65,193},{129,1},{193,65... | collective-permute-start | bytes 196616 | tf_op jit(solution)/shard_map/ppermute | solution.py:238
  169.2 4.3 %collective-permute-start.17 = (bf16[4,2,16,256]{3,2,1,0:T(8,128)(2,1)S(1)}, bf16[4,2,16,256]{3,2,1,0:T(8,128)(2,1)S(1)}, u32[]{:S(2)}, u32[]{:S(2)}) collective-permute-start(bf16[4,2,16,256]{3,2,1,0:T(8,128)(2,1)S(1)} %get-tuple-element.71), channel_id=1, source_target_pairs={{0,192},{64,0},{128,64},{192,128},{1,193},{65,1},{129,65},{193,129... | collective-permute-start | bytes 196616 | tf_op jit(solution)/shard_map/ppermute | solution.py:238
  208.7 6.2 %collective-permute-start.18 = (bf16[4,2,16,256]{3,2,1,0:T(8,128)(2,1)S(1)}, bf16[4,2,16,256]{3,2,1,0:T(8,128)(2,1)S(1)}, u32[]{:S(2)}, u32[]{:S(2)}) collective-permute-start(bf16[4,2,16,256]{3,2,1,0:T(8,128)(2,1)S(1)} %get-tuple-element.73), channel_id=1, source_target_pairs={{0,64},{64,128},{128,192},{192,0},{1,65},{65,129},{129,193},{193,1... | collective-permute-start | bytes 196616 | tf_op jit(solution)/shard_map/ppermute | solution.py:238
  208.8 7.0 %collective-permute-start.19 = (bf16[4,2,16,256]{3,2,1,0:T(8,128)(2,1)S(1)}, bf16[4,2,16,256]{3,2,1,0:T(8,128)(2,1)S(1)}, u32[]{:S(2)}, u32[]{:S(2)}) collective-permute-start(bf16[4,2,16,256]{3,2,1,0:T(8,128)(2,1)S(1)} %get-tuple-element.74), channel_id=1, source_target_pairs={{0,128},{64,192},{128,0},{192,64},{1,129},{65,193},{129,1},{193,65... | collective-permute-start | bytes 196616 | tf_op jit(solution)/shard_map/ppermute | solution.py:238
  211.7 5.4 %collective-permute-start.20 = (bf16[4,2,16,256]{3,2,1,0:T(8,128)(2,1)S(1)}, bf16[4,2,16,256]{3,2,1,0:T(8,128)(2,1)S(1)}, u32[]{:S(2)}, u32[]{:S(2)}) collective-permute-start(bf16[4,2,16,256]{3,2,1,0:T(8,128)(2,1)S(1)} %get-tuple-element.75), channel_id=1, source_target_pairs={{0,192},{64,0},{128,64},{192,128},{1,193},{65,1},{129,65},{193,129... | collective-permute-start | bytes 196616 | tf_op jit(solution)/shard_map/ppermute | solution.py:238
  218.6 5.6 %collective-permute-start.21 = (bf16[4,2,16,256]{3,2,1,0:T(8,128)(2,1)S(1)}, bf16[4,2,16,256]{3,2,1,0:T(8,128)(2,1)S(1)}, u32[]{:S(2)}, u32[]{:S(2)}) collective-permute-start(bf16[4,2,16,256]{3,2,1,0:T(8,128)(2,1)S(1)} %get-tuple-element.77), channel_id=1, source_target_pairs={{0,64},{64,128},{128,192},{192,0},{1,65},{65,129},{129,193},{193,1... | collective-permute-start | bytes 196616 | tf_op jit(solution)/shard_map/ppermute | solution.py:238
  219.7 6.7 %collective-permute-start.22 = (bf16[4,2,16,256]{3,2,1,0:T(8,128)(2,1)S(1)}, bf16[4,2,16,256]{3,2,1,0:T(8,128)(2,1)S(1)}, u32[]{:S(2)}, u32[]{:S(2)}) collective-permute-start(bf16[4,2,16,256]{3,2,1,0:T(8,128)(2,1)S(1)} %get-tuple-element.78), channel_id=1, source_target_pairs={{0,128},{64,192},{128,0},{192,64},{1,129},{65,193},{129,1},{193,65... | collective-permute-start | bytes 196616 | tf_op jit(solution)/shard_map/ppermute | solution.py:238
  222.9 4.3 %collective-permute-start.23 = (bf16[4,2,16,256]{3,2,1,0:T(8,128)(2,1)S(1)}, bf16[4,2,16,256]{3,2,1,0:T(8,128)(2,1)S(1)}, u32[]{:S(2)}, u32[]{:S(2)}) collective-permute-start(bf16[4,2,16,256]{3,2,1,0:T(8,128)(2,1)S(1)} %get-tuple-element.79), channel_id=1, source_target_pairs={{0,192},{64,0},{128,64},{192,128},{1,193},{65,1},{129,65},{193,129... | collective-permute-start | bytes 196616 | tf_op jit(solution)/shard_map/ppermute | solution.py:238
